TPU v7x, 256 devices: a whole 4x4x8 slice. The times are simulated.
256 devices in a mesh: img: 4 (over x_lo, core), txt: 64 (over y, z, x_hi).
Axes of the slice: x: 4 (x_hi: 2, x_lo: 2; x = x_hi * 2 + x_lo), y: 4, z: 8, core: 2. Of those that a mesh axis runs over, the one named last changes fastest.
Arguments:
- images: bfloat16 [14336, 1280], P(('img', 'txt')), may hold values from -128 to 128
- texts: bfloat16 [14336, 1280], P(('txt', 'img')), may hold values from -16 to 16
- logit_scale: float32 [1], replicated, may hold values from 0.02 to 0.04
Outputs:
- loss: float32 [1], replicated
- image_grad: float32 [14336, 1280], P(('img', 'txt'))
- text_grad: float32 [14336, 1280], P(('txt', 'img'))
All inputs are finite; a program needn't handle non-finite values.
Results may differ from a plain program's by a relative error of at most 0.0021.
Values may be sent and summed in bfloat16 or wider, within the bound.
A program may use at most 64 MiB of HBM per device.

v0:
```python
import jax
import jax.numpy as jnp
from jax import lax
from jax.sharding import PartitionSpec as P


def per_device(images, texts, logit_scale):
    scale = logit_scale[0]
    own_rows = images.shape[0]
    img_place = lax.axis_index("img")
    txt_place = lax.axis_index("txt")
    img_count = lax.axis_size("img")
    txt_count = lax.axis_size("txt")
    text_tile = lax.all_gather(texts, "img", axis=0, tiled=True)
    image_tile = lax.all_gather(images, "txt", axis=0, tiled=True)
    logits = scale * lax.dot_general(
        image_tile, text_tile, (((1,), (1,)), ((), ())), preferred_element_type=jnp.float32
    )
    row_peak = lax.pmax(jnp.max(logits, 1), "txt")
    col_peak = lax.pmax(jnp.max(logits, 0), "img")
    row_total = lax.psum(jnp.sum(jnp.exp(logits - row_peak[:, None]), 1), "txt")
    col_total = lax.psum(jnp.sum(jnp.exp(logits - col_peak[None, :]), 0), "img")
    row_ids = img_place * image_tile.shape[0] + jnp.arange(image_tile.shape[0], dtype=jnp.int32)
    col_ids = txt_place * text_tile.shape[0] + jnp.arange(text_tile.shape[0], dtype=jnp.int32)
    row_start = txt_place * own_rows
    col_start = img_place * own_rows
    on_diagonal = row_ids[:, None] == col_ids[None, :]
    row_prob = jnp.exp(logits - row_peak[:, None]) / row_total[:, None]
    col_prob = jnp.exp(logits - col_peak[None, :]) / col_total[None, :]
    weights = (0.5 * (row_prob + col_prob) - jnp.where(on_diagonal, 1.0, 0.0)).astype(jnp.bfloat16)
    row_lse = lax.dynamic_slice_in_dim(row_peak + jnp.log(row_total), row_start, own_rows)
    col_lse = lax.dynamic_slice_in_dim(col_peak + jnp.log(col_total), col_start, own_rows)
    diagonal_sum = jnp.sum(jnp.where(on_diagonal, logits, 0.0))
    local_term = jnp.sum(row_lse) + jnp.sum(col_lse) - 2.0 * diagonal_sum
    total = lax.psum(local_term, ("img", "txt"))
    pairs = own_rows * img_count * txt_count
    loss = jnp.reshape(total / (2.0 * pairs), (1,))
    text_terms = lax.dot_general(
        weights, image_tile, (((0,), (0,)), ((), ())), preferred_element_type=jnp.float32
    )
    text_grad = lax.psum_scatter(text_terms, "img", scatter_dimension=0, tiled=True)
    image_terms = jnp.dot(weights, text_tile, preferred_element_type=jnp.float32)
    image_grad = lax.psum_scatter(image_terms, "txt", scatter_dimension=0, tiled=True)
    return (loss, image_grad, text_grad)


def solution(mesh):
    in_specs = (P(("img", "txt"), None), P(("txt", "img"), None), P())
    out_specs = (P(), P(("img", "txt"), None), P(("txt", "img"), None))
    return jax.shard_map(
        per_device, mesh=mesh, in_specs=in_specs, out_specs=out_specs, check_vma=False
    )
```

profile of v0, /device:TPU:1, one launch (start us, length us, event | category | flops | bytes accessed | tf_op | source)
XLA Modules:
  0.0 1336.4 jit_solution(7417664394297845504)
XLA Ops:
  7.2 0.0 all-gather.2.cloned.1.call-start
  7.2 0.7 all-gather.2.cloned.1.call-update
  7.9 0.0 reduce-scatter.5.cloned.1.call-start
  8.6 10.4 all_gather.7
  19.0 150.5 %all-gather.2.cloned.1.call-done = bf16[3584,1280]{1,0:T(8,128)(2,1)} async-done(((bf16[56,1280]{1,0:T(8,128)(2,1)}), bf16[3584,1280]{1,0:T(8,128)(2,1)}) %all-gather.2.cloned.1.call-update) | async-done | bytes 9175056 | tf_op jit(solution)/shard_map/all_gather | solution.py:15
  169.5 6.6 fusion.10
  176.1 7.1 pmax.15
  183.1 299.9 %pmax.14 = f32[3584]{0:T(1024)S(1)} all-reduce(f32[3584]{0:T(1024)S(1)} %get-tuple-element.7), channel_id=1, replica_groups=mesh['img'=4,'txt'=64] {'txt'}, use_global_device_ids=true, to_apply=%region_1.0 | all-reduce | flops 3584 | bytes 28672 | tf_op jit(solution)/shard_map/pmax | solution.py:19
  483.0 2.4 fusion
  485.5 60.7 %psum.22 = f32[224]{0:T(256)S(1)} all-reduce(f32[224]{0:T(256)S(1)} %get-tuple-element.4), channel_id=1, replica_groups=mesh['img'=4,'txt'=64] {'img'}, use_global_device_ids=true, to_apply=%region_8.9 | all-reduce | flops 224 | bytes 1792 | tf_op jit(solution)/shard_map/psum | solution.py:22
  546.2 296.6 %psum.21 = f32[3584]{0:T(1024)S(1)} all-reduce(f32[3584]{0:T(1024)S(1)} %get-tuple-element.5), channel_id=1, replica_groups=mesh['img'=4,'txt'=64] {'txt'}, use_global_device_ids=true, to_apply=%region_3.0 | all-reduce | flops 3584 | bytes 28672 | tf_op jit(solution)/shard_map/psum | solution.py:21
  842.8 7.9 fusion.6
  850.7 0.0 reduce-scatter.5.cloned.1.call-update
  850.7 0.0 reduce-scatter.3.cloned.1.call-start
  850.7 9.4 fusion.8
  860.2 0.0 reduce-scatter.3.cloned.1.call-update
  860.8 0.8 dynamic-slice_reduce_fusion
  861.6 0.7 fusion.5
  863.6 132.8 %psum.23 = f32[]{:T(128)} all-reduce(f32[]{:T(128)S(6)} %sub.16), channel_id=1, replica_groups=mesh['img'=4,'txt'=64] {'img','txt'}, use_global_device_ids=true, to_apply=%region_11.12 | all-reduce | flops 1 | bytes 8 | tf_op jit(solution)/shard_map/psum | solution.py:35
  997.0 0.0 reduce-scatter.5.cloned.1.call-done
  997.1 331.7 %reduce-scatter.3.cloned.1.call-done = f32[56,1280]{1,0:T(8,128)} async-done(((f32[3584,1280]{1,0:T(8,128)}), f32[56,1280]{1,0:T(8,128)}) %reduce-scatter.3.cloned.1.call-update) | async-done | bytes 286736 | tf_op jit(solution)/shard_map/reduce_scatter | solution.py:43
  (3 shorter events, 0.0 us)
Async XLA Ops:
  7.2 162.3 %all-gather.2.cloned.1.call-start = ((), (), s32[]{:S(2)}) async-start(), calls=%async_computation.2 | async-start | bytes 9318400 | tf_op jit(solution)/shard_map/all_gather | solution.py:15
  7.9 989.1 %reduce-scatter.5.cloned.1.call-start = ((), (), s32[]{:S(2)}) async-start(), calls=%async_computation.4 | async-start | bytes 1433600 | tf_op jit(solution)/shard_map/reduce_scatter | solution.py:41
  850.7 478.1 %reduce-scatter.3.cloned.1.call-start = ((), (), s32[]{:S(2)}) async-start(), calls=%async_computation.3 | async-start | bytes 18636800 | tf_op jit(solution)/shard_map/reduce_scatter | solution.py:43
Sparse Core Ops, SparseCore 0:
  11.6 157.8 all-gather.1
  850.8 70.3 reduce-scatter.4
  924.4 404.3 reduce-scatter.2
where the time goes:
time: 1340 us
  blocking collectives  807 us (60%)
  waiting for transfers between devices  483 us (36%)
  matrix products  23.9 us (2%)
  between operations  18.2 us (1%)
    reduce_scatter x1, waiting for transfers between devices, per_device(): lax.psum_scatter(image_terms, 'txt', scatter_dimension=0, tiled=True)  332 us
    pmax x1, blocking collectives, per_device(): row_peak = lax.pmax(jnp.max(logits, 1), 'txt')  300 us
    psum x1, blocking collectives, per_device(): row_total = lax.psum(jnp.sum(jnp.exp(logits - row_peak[:, None]), 1), 'txt')  297 us
    all_gather x1, waiting for transfers between devices, per_device(): image_tile = lax.all_gather(images, 'txt', axis=0, tiled=True)  150 us
    psum x1, blocking collectives, per_device(): total = lax.psum(local_term, ('img', 'txt'))  133 us
    psum x1, blocking collectives, per_device(): col_total = lax.psum(jnp.sum(jnp.exp(logits - col_peak[None, :]), 0), 'img')  60.7 us
  transfers between devices with their start and end apart: 3, of which 2 were waited for; matrix products, arithmetic and copies ran while one was open for 1% of the time, Pallas kernels for 0%

commit v1 on v0

v1 whole, which is shorter than its diff:
```python
import functools

import jax
import jax.numpy as jnp
from jax import lax
from jax.experimental import pallas as pl
from jax.experimental.pallas import tpu as pltpu
from jax.sharding import PartitionSpec as P

MESH = pl.DeviceIdType.MESH
ROWS = 56
PITCH = 64
SIDE = 16
TILE = SIDE * PITCH
E = 1280
PAIRS = 14336
WIDE = 256
FLOOR = -1e30
PIECES = (
    (0, 0, 256, 0),
    (1, 256, 256, 0),
    (0, 512, 256, 256),
    (1, 768, 256, 256),
    (0, 1024, 128, 512),
    (1, 1152, 128, 512),
)
HALF = 640


def device(x, y, z, c):
    return (lax.rem(x, 2) * 2 + c, (y * 8 + z) * 2 + lax.div(x, 2))


def kernel(
    images_ref, texts_ref, scale_ref,
    loss_ref, igrad_ref, tgrad_ref,
    ibuf, tbuf, ibig, tbig, logits, prow, pcol, weights, wturned,
    rsub, csum, cmax, dsum, frow, rmsg, cmsg, rstats, cstats, lmsg, lstats, pmsg, pstats,
    xout, xin, zacc, zout, zin, tacc, sout, sin, pout, pin, pkeep,
    zsend, isend, irecv, tsend0, trecv, tsend1,
    rsend, rrecv, csend, crecv, lsend, lrecv, psend, precv,
    xsend, xrecv, zosend, zorecv, ssend, srecv, ppsend, pprecv,
):
    img = lax.axis_index("img")
    txt = lax.axis_index("txt")
    x_lo = lax.div(img, 2)
    c = lax.rem(img, 2)
    x_hi = lax.rem(txt, 2)
    x = x_hi * 2 + x_lo
    y = lax.div(txt, 16)
    z = lax.rem(lax.div(txt, 2), 8)
    oc = 1 - c
    islot = c * 8 + z
    tslot = x * 4 + y

    def row_peer(slot):
        return device(x, y, lax.rem(slot, 8), lax.div(slot, 8))

    def col_peer(slot):
        return device(lax.div(slot, 4), lax.rem(slot, 4), z, c)

    def copy(src, dst, send, recv, where):
        return pltpu.make_async_remote_copy(
            src_ref=src, dst_ref=dst, send_sem=send, recv_sem=recv,
            device_id=where, device_id_type=MESH,
        )

    barrier = pltpu.get_barrier_semaphore()

    def greet(k, carry):
        pl.semaphore_signal(barrier, inc=1, device_id=row_peer(lax.rem(islot + k, SIDE)), device_id_type=MESH)
        pl.semaphore_signal(barrier, inc=1, device_id=col_peer(lax.rem(tslot + k, SIDE)), device_id_type=MESH)
        return carry

    lax.fori_loop(1, SIDE, greet, 0)
    ibuf[islot] = images_ref[...]
    tbuf[tslot] = texts_ref[...]
    ibig[...] = jnp.zeros_like(ibig)
    tbig[...] = jnp.zeros_like(tbig)
    weights[...] = jnp.zeros_like(weights)
    rsub[...] = jnp.zeros_like(rsub)
    pl.semaphore_wait(barrier, 2 * (SIDE - 1))

    def z_copy(owner, way, step):
        slot = c * 8 + owner
        there = lax.rem(z + (1 if way == 0 else 7), 8)
        return copy(ibuf.at[slot], ibuf.at[slot], zsend.at[way, step], irecv.at[slot], device(x, y, there, c))

    def cross_copy(slot, k):
        return copy(ibuf.at[slot], ibuf.at[slot], isend.at[k], irecv.at[slot], device(x, y, z, oc))

    def wait_image(slot):
        copy(ibuf.at[slot], ibuf.at[slot], isend.at[0], irecv.at[slot], device(x, y, z, oc)).wait_recv()

    def whole_copy(axis, d):
        there = device(lax.rem(x + d, 4), y, z, c) if axis == 0 else device(x, lax.rem(y + d, 4), z, c)
        return copy(tbuf.at[tslot], tbuf.at[tslot], tsend0.at[axis, d], trecv.at[0, tslot], there)

    def wait_whole(slot):
        copy(tbuf.at[slot], tbuf.at[slot], tsend0.at[0, 0], trecv.at[0, slot], device(x, y, z, oc)).wait_recv()

    def half_ref(slot, half):
        return tbuf.at[slot, :, pl.ds(half * HALF, HALF)]

    def half_copy(half, d, e):
        if half == 0:
            slot = lax.rem(x + d, 4) * 4 + y
            there = device(x, lax.rem(y + e, 4), z, c)
        else:
            slot = x * 4 + lax.rem(y + d, 4)
            there = device(lax.rem(x + e, 4), y, z, c)
        return copy(half_ref(slot, half), half_ref(slot, half), tsend1.at[half, d * 4 + e], trecv.at[half, slot], there)

    def wait_half(slot, half):
        copy(half_ref(slot, half), half_ref(slot, half), tsend0.at[0, 0], trecv.at[half, slot], device(x, y, z, oc)).wait_recv()

    z_copy(z, 0, 0).start()
    z_copy(z, 1, 0).start()
    for d in (1, 3, 2):
        whole_copy(0, d).start()
        whole_copy(1, d).start()
    cross_copy(islot, 0).start()

    def place_image(slot):
        at = pl.multiple_of(slot * PITCH, PITCH)
        ibig[pl.ds(at, ROWS), :] = ibuf[slot]

    def place_text(slot):
        at = pl.multiple_of(slot * PITCH, PITCH)
        tbig[pl.ds(at, ROWS), :] = tbuf[slot]

    place_image(islot)
    place_text(tslot)
    for step in range(3):
        left = lax.rem(z + 7 - step, 8)
        right = lax.rem(z + 1 + step, 8)
        wait_image(c * 8 + left)
        if step < 2:
            z_copy(left, 0, step + 1).start()
        else:
            @pl.when(c == 0)
            def _():
                z_copy(left, 0, 3).start()
        cross_copy(c * 8 + left, 1 + step).start()
        wait_image(c * 8 + right)
        if step < 2:
            z_copy(right, 1, step + 1).start()
        else:
            @pl.when(c == 1)
            def _():
                z_copy(right, 1, 3).start()
        cross_copy(c * 8 + right, 4 + step).start()
        d = (1, 3, 2)[step]
        slot0 = lax.rem(x + d, 4) * 4 + y
        slot1 = x * 4 + lax.rem(y + d, 4)
        wait_whole(slot0)
        wait_whole(slot1)
        for e in (1, 3, 2):
            half_copy(0, d, e).start()
            half_copy(1, d, e).start()
        place_image(c * 8 + left)
        place_image(c * 8 + right)
        place_text(slot0)
        place_text(slot1)
    far = lax.rem(z + 4, 8)
    wait_image(c * 8 + far)
    cross_copy(c * 8 + far, 7).start()
    place_image(c * 8 + far)
    for d in (1, 3, 2):
        for e in (1, 3, 2):
            slot = lax.rem(x + d, 4) * 4 + lax.rem(y + e, 4)
            wait_half(slot, 0)
            wait_half(slot, 1)
            place_text(slot)

    def other_image(k, carry):
        slot = oc * 8 + k
        wait_image(slot)
        place_image(slot)
        return carry

    lax.fori_loop(0, 8, other_image, 0)

    scale = scale_ref[0]
    lane = lax.broadcasted_iota(jnp.int32, (1, TILE), 1)
    inside = lax.bitwise_and(lane, PITCH - 1)
    block = lax.shift_right_logical(lane, 6)
    block_x = lax.shift_right_logical(block, 2)
    block_y = lax.bitwise_and(block, 3)
    col_block = ((block_y * 8 + z) * 2 + lax.shift_right_logical(block_x, 1)) * 4 + lax.bitwise_and(block_x, 1) * 2 + c
    col_id = jnp.where(inside < ROWS, col_block * ROWS + inside, -1)

    def score(n, carry):
        cols = pl.ds(pl.multiple_of(n * WIDE, WIDE), WIDE)
        part = lax.dot_general(
            ibig[...], tbig[cols, :], (((1,), (1,)), ((), ())), preferred_element_type=jnp.float32
        )
        pad = lax.bitwise_and(lax.broadcasted_iota(jnp.int32, (1, WIDE), 1), PITCH - 1) >= ROWS
        logits[:, cols] = jnp.where(pad, FLOOR, part * scale)
        return carry

    lax.fori_loop(0, TILE // WIDE, score, 0)

    def rows_of(k):
        return pl.ds(pl.multiple_of(k * PITCH, PITCH), ROWS)

    cmax[...] = jnp.full_like(cmax, FLOOR)

    def col_max(k, carry):
        cmax[...] = jnp.maximum(cmax[...], jnp.max(logits[rows_of(k), :].reshape(7, 8, TILE), 0))
        return carry

    lax.fori_loop(0, SIDE, col_max, 0)
    col_top = jnp.max(cmax[...], 0, keepdims=True)
    csum[...] = jnp.zeros_like(csum)
    dsum[...] = jnp.zeros_like(dsum)

    def on_diagonal(k):
        row_block = (x_lo * 2 + lax.div(k, 8)) * 64 + (y * 8 + lax.rem(k, 8)) * 2 + x_hi
        row_id = row_block * ROWS + lax.broadcasted_iota(jnp.int32, (ROWS, 1), 0)
        return row_id == col_id

    def exponentials(k, carry):
        part = logits[rows_of(k), :]
        top = jnp.max(part, 1, keepdims=True)
        by_row = jnp.exp(part - top)
        by_col = jnp.exp(part - col_top)
        prow[rows_of(k), :] = by_row
        pcol[rows_of(k), :] = by_col
        total = jnp.sum(by_row, 1, keepdims=True)
        first = lax.broadcasted_iota(jnp.int32, (ROWS, 128), 1) == 0
        rsub[rows_of(k), :] = jnp.where(first, top, total)
        csum[...] += jnp.sum(by_col.reshape(7, 8, TILE), 0)
        dsum[...] += jnp.sum(jnp.where(on_diagonal(k), part, 0.0).reshape(7, 8, TILE), 0)
        return carry

    lax.fori_loop(0, SIDE, exponentials, 0)

    row_stats = jnp.transpose(rsub[...], (1, 0))
    col_total_here = jnp.sum(csum[...], 0, keepdims=True)
    for k in range(4):
        part = slice(k * WIDE, (k + 1) * WIDE)
        rmsg[k:k + 1, :] = row_stats[0:1, part]
        rmsg[4 + k:5 + k, :] = row_stats[1:2, part]
        cmsg[k:k + 1, :] = col_top[:, part]
        cmsg[4 + k:5 + k, :] = col_total_here[:, part]
    rstats[islot] = rmsg[...]
    cstats[tslot] = cmsg[...]

    def row_stat_copy(peer):
        return copy(rmsg, rstats.at[islot], rsend.at[peer], rrecv.at[islot], row_peer(peer))

    def col_stat_copy(peer):
        return copy(cmsg, cstats.at[tslot], csend.at[peer], crecv.at[tslot], col_peer(peer))

    def send_stats(k, carry):
        row_stat_copy(lax.rem(islot + k, SIDE)).start()
        col_stat_copy(lax.rem(tslot + k, SIDE)).start()
        return carry

    lax.fori_loop(1, SIDE, send_stats, 0)

    def take_stats(k, carry):
        peer = lax.rem(islot + k, SIDE)
        copy(rmsg, rstats.at[peer], rsend.at[peer], rrecv.at[peer], row_peer(peer)).wait_recv()
        peer = lax.rem(tslot + k, SIDE)
        copy(cmsg, cstats.at[peer], csend.at[peer], crecv.at[peer], col_peer(peer)).wait_recv()
        return carry

    lax.fori_loop(1, SIDE, take_stats, 0)

    def combine(stats, mine):
        peaks = stats[:, 0:4, :]
        totals = stats[:, 4:8, :]
        peak = jnp.max(peaks, 0)
        total = jnp.sum(totals * jnp.exp(peaks - peak[None]), 0)
        factor = 0.5 * jnp.exp(mine[0:4, :] - peak) / total
        return peak + jnp.log(total), factor

    row_lse, row_factor = combine(rstats, rmsg)
    col_lse, col_factor = combine(cstats, cmsg)

    def line(v):
        return jnp.concatenate([v[k:k + 1, :] for k in range(4)], 1)

    col_line = line(col_factor)
    frow[...] = jnp.transpose(jnp.broadcast_to(line(row_factor), (128, TILE)), (1, 0))

    def weigh(k, carry):
        factor = frow[rows_of(k), :][:, 0:1]
        w = factor * prow[rows_of(k), :] + col_line * pcol[rows_of(k), :]
        w = w - jnp.where(on_diagonal(k), 1.0, 0.0)
        weights[rows_of(k), :] = w.astype(jnp.bfloat16)
        return carry

    lax.fori_loop(0, SIDE, weigh, 0)

    def cross_term(n):
        cols = pl.ds(pl.multiple_of(n * WIDE, WIDE), WIDE)
        return copy(xout.at[:, :, cols], xin.at[:, :, cols], xsend.at[n], xrecv.at[n], device(x, y, z, oc))

    def other_terms(n, carry):
        cols = pl.ds(pl.multiple_of(n * WIDE, WIDE), WIDE)
        at = pl.multiple_of(oc * (8 * PITCH), 8 * PITCH)
        part = jnp.dot(weights[pl.ds(at, 8 * PITCH), :], tbig[:, cols], preferred_element_type=jnp.float32)
        for m in range(8):
            xout[m, :, cols] = part[m * PITCH:m * PITCH + ROWS]
        cross_term(n).start()
        return carry

    lax.fori_loop(0, E // WIDE, other_terms, 0)

    def z_term(n, d):
        cols = pl.ds(pl.multiple_of(n * WIDE, WIDE), WIDE)
        there = lax.rem(z + d, 8)
        return copy(zout.at[there, :, cols], zin.at[z, :, cols], zosend.at[n, d], zorecv.at[n, z], device(x, y, there, c))

    def z_wait(n, d):
        cols = pl.ds(pl.multiple_of(n * WIDE, WIDE), WIDE)
        src = lax.rem(z + d, 8)
        copy(zin.at[src, :, cols], zin.at[src, :, cols], zosend.at[n, d], zorecv.at[n, src], device(x, y, z, oc)).wait_recv()

    def own_terms(n, carry):
        cols = pl.ds(pl.multiple_of(n * WIDE, WIDE), WIDE)
        at = pl.multiple_of(c * (8 * PITCH), 8 * PITCH)
        part = jnp.dot(weights[pl.ds(at, 8 * PITCH), :], tbig[:, cols], preferred_element_type=jnp.float32)
        cross_term(n).wait_recv()
        for m in range(8):
            both = part[m * PITCH:m * PITCH + ROWS] + xin[m, :, cols]
            zacc[m, :, cols] = both
            zout[m, :, cols] = both.astype(jnp.bfloat16)
        for d in (4, 3, 5, 2, 6, 1, 7):
            z_term(n, d).start()
        return carry

    lax.fori_loop(0, E // WIDE, own_terms, 0)

    for k in range(TILE // 128):
        wturned[:, k * 128:(k + 1) * 128] = jnp.transpose(weights[k * 128:(k + 1) * 128, :], (1, 0))

    def first_peer(axis, f):
        return device(x, f, z, c) if axis == 0 else device(f, y, z, c)

    def second_peer(axis, s):
        return device(s, y, z, c) if axis == 0 else device(x, s, z, c)

    def slab_copy(p, d):
        axis, _, width, at = PIECES[p]
        me = y if axis == 0 else x
        there = lax.rem(me + d, 4)
        return copy(
            sout.at[axis, there, :, :, pl.ds(at, width)], sin.at[axis, me, :, :, pl.ds(at, width)],
            ssend.at[p, d], srecv.at[p, me], first_peer(axis, there),
        )

    def slab_wait(p, d):
        axis, _, width, at = PIECES[p]
        me = y if axis == 0 else x
        src = lax.rem(me + d, 4)
        ref = sin.at[axis, src, :, :, pl.ds(at, width)]
        copy(ref, ref, ssend.at[p, d], srecv.at[p, src], first_peer(axis, src)).wait_recv()

    for n in range(E // WIDE):
        part = jnp.dot(wturned[...], ibig[:, n * WIDE:(n + 1) * WIDE], preferred_element_type=jnp.float32)
        for p, (axis, col, width, at) in enumerate(PIECES):
            if col // WIDE != n:
                continue
            for m in range(SIDE):
                piece = part[m * PITCH:m * PITCH + ROWS, col - n * WIDE:col - n * WIDE + width]
                tacc[m, :, col:col + width] = piece
                first, second = (m % 4, m // 4) if axis == 0 else (m // 4, m % 4)
                sout[axis, first, second, :, at:at + width] = piece.astype(jnp.bfloat16)
            for d in (2, 1, 3):
                slab_copy(p, d).start()

    index = lax.broadcasted_iota(jnp.int32, (4, WIDE), 0) * WIDE + lax.broadcasted_iota(jnp.int32, (4, WIDE), 1)
    slot_of = lax.shift_right_logical(index, 6)
    valid = lax.bitwise_and(index, PITCH - 1) < ROWS
    terms = jnp.where(valid & (slot_of == islot), row_lse, 0.0) + jnp.where(valid & (slot_of == tslot), col_lse, 0.0)
    term = jnp.sum(jnp.sum(terms, 0, keepdims=True), 1, keepdims=True)
    diagonal = jnp.sum(jnp.sum(dsum[...], 0, keepdims=True), 1, keepdims=True)
    lmsg[...] = jnp.broadcast_to(term - 2.0 * diagonal, (8, 128))
    lstats[islot] = lmsg[...]

    def send_loss(k, carry):
        peer = lax.rem(islot + k, SIDE)
        copy(lmsg, lstats.at[islot], lsend.at[peer], lrecv.at[islot], row_peer(peer)).start()
        return carry

    lax.fori_loop(1, SIDE, send_loss, 0)

    def keep_copy(p, d):
        axis, _, width, at = PIECES[p]
        me = x if axis == 0 else y
        there = lax.rem(me + d, 4)
        return copy(
            pout.at[axis, there, :, pl.ds(at, width)], pin.at[axis, me, :, pl.ds(at, width)],
            ppsend.at[p, d], pprecv.at[p, me], second_peer(axis, there),
        )

    for p, (axis, col, width, at) in enumerate(PIECES):
        for d in (1, 3, 2):
            slab_wait(p, d)
        me1 = y if axis == 0 else x
        me2 = x if axis == 0 else y
        for d in (2, 1, 3, 0):
            s = lax.rem(me2 + d, 4)
            m = s * 4 + y if axis == 0 else x * 4 + s
            total = tacc[m, :, col:col + width]
            for e in (1, 2, 3):
                f = lax.rem(me1 + e, 4)
                total = total + sin[axis, f, s, :, at:at + width].astype(jnp.float32)
            if d == 0:
                pkeep[:, col:col + width] = total
            else:
                pout[axis, s, :, at:at + width] = total.astype(jnp.bfloat16)
                keep_copy(p, d).start()

    def take_loss(k, carry):
        peer = lax.rem(islot + k, SIDE)
        copy(lmsg, lstats.at[peer], lsend.at[peer], lrecv.at[peer], row_peer(peer)).wait_recv()
        return carry

    lax.fori_loop(1, SIDE, take_loss, 0)
    pmsg[...] = jnp.sum(lstats[...], 0)
    pstats[tslot] = pmsg[...]

    def send_sum(k, carry):
        peer = lax.rem(tslot + k, SIDE)
        copy(pmsg, pstats.at[tslot], psend.at[peer], precv.at[tslot], col_peer(peer)).start()
        return carry

    lax.fori_loop(1, SIDE, send_sum, 0)

    for p, (axis, col, width, at) in enumerate(PIECES):
        me = x if axis == 0 else y
        total = pkeep[:, col:col + width]
        for d in (1, 3, 2):
            src = lax.rem(me + d, 4)
            ref = pin.at[axis, src, :, pl.ds(at, width)]
            copy(ref, ref, ppsend.at[p, d], pprecv.at[p, src], second_peer(axis, src)).wait_recv()
            total = total + pin[axis, src, :, at:at + width].astype(jnp.float32)
        tgrad_ref[:, col:col + width] = total

    def image_result(n, carry):
        cols = pl.ds(pl.multiple_of(n * WIDE, WIDE), WIDE)
        total = zacc[z, :, cols]
        for d in (1, 7, 2, 6, 3, 5, 4):
            z_wait(n, d)
            total = total + zin[lax.rem(z + d, 8), :, cols].astype(jnp.float32)
        igrad_ref[:, cols] = total
        return carry

    lax.fori_loop(0, E // WIDE, image_result, 0)

    def take_sum(k, carry):
        peer = lax.rem(tslot + k, SIDE)
        copy(pmsg, pstats.at[peer], psend.at[peer], precv.at[peer], col_peer(peer)).wait_recv()
        return carry

    lax.fori_loop(1, SIDE, take_sum, 0)
    loss = jnp.sum(pstats[...], 0) / (2.0 * PAIRS)
    loss_ref[0] = loss[0, 0]

    for way in range(2):
        for step in range(3):
            z_copy(z, way, step).wait_send()

    @pl.when(c == 0)
    def _():
        z_copy(z, 0, 3).wait_send()

    @pl.when(c == 1)
    def _():
        z_copy(z, 1, 3).wait_send()

    for k in range(8):
        cross_copy(islot, k).wait_send()
    for d in (1, 3, 2):
        whole_copy(0, d).wait_send()
        whole_copy(1, d).wait_send()
        for e in (1, 3, 2):
            half_copy(0, d, e).wait_send()
            half_copy(1, d, e).wait_send()

    def sent(k, carry):
        peer = lax.rem(islot + k, SIDE)
        row_stat_copy(peer).wait_send()
        copy(lmsg, lstats.at[islot], lsend.at[peer], lrecv.at[islot], row_peer(peer)).wait_send()
        peer = lax.rem(tslot + k, SIDE)
        col_stat_copy(peer).wait_send()
        copy(pmsg, pstats.at[tslot], psend.at[peer], precv.at[tslot], col_peer(peer)).wait_send()
        return carry

    lax.fori_loop(1, SIDE, sent, 0)

    def terms_sent(n, carry):
        cross_term(n).wait_send()
        for d in range(1, 8):
            z_term(n, d).wait_send()
        return carry

    lax.fori_loop(0, E // WIDE, terms_sent, 0)
    for p in range(len(PIECES)):
        for d in (1, 2, 3):
            slab_copy(p, d).wait_send()
            keep_copy(p, d).wait_send()


def per_device(images, texts, logit_scale):
    f32, bf16 = jnp.float32, jnp.bfloat16
    dma = pltpu.SemaphoreType.DMA
    vmem = pl.BlockSpec(memory_space=pltpu.VMEM)
    smem = pl.BlockSpec(memory_space=pltpu.SMEM)
    loss, image_grad, text_grad = pl.pallas_call(
        kernel,
        out_shape=(
            jax.ShapeDtypeStruct((1,), f32),
            jax.ShapeDtypeStruct((ROWS, E), f32),
            jax.ShapeDtypeStruct((ROWS, E), f32),
        ),
        in_specs=[vmem, vmem, smem],
        out_specs=(smem, vmem, vmem),
        scratch_shapes=[
            pltpu.VMEM((SIDE, ROWS, E), bf16),
            pltpu.VMEM((SIDE, ROWS, E), bf16),
            pltpu.VMEM((TILE, E), bf16),
            pltpu.VMEM((TILE, E), bf16),
            pltpu.VMEM((TILE, TILE), f32),
            pltpu.VMEM((TILE, TILE), f32),
            pltpu.VMEM((TILE, TILE), f32),
            pltpu.VMEM((TILE, TILE), bf16),
            pltpu.VMEM((TILE, TILE), bf16),
            pltpu.VMEM((TILE, 128), f32),
            pltpu.VMEM((8, TILE), f32),
            pltpu.VMEM((8, TILE), f32),
            pltpu.VMEM((8, TILE), f32),
            pltpu.VMEM((TILE, 128), f32),
            pltpu.VMEM((8, WIDE), f32),
            pltpu.VMEM((8, WIDE), f32),
            pltpu.VMEM((SIDE, 8, WIDE), f32),
            pltpu.VMEM((SIDE, 8, WIDE), f32),
            pltpu.VMEM((8, 128), f32),
            pltpu.VMEM((SIDE, 8, 128), f32),
            pltpu.VMEM((8, 128), f32),
            pltpu.VMEM((SIDE, 8, 128), f32),
            pltpu.VMEM((8, ROWS, E), f32),
            pltpu.VMEM((8, ROWS, E), f32),
            pltpu.VMEM((8, ROWS, E), f32),
            pltpu.VMEM((8, ROWS, E), bf16),
            pltpu.VMEM((8, ROWS, E), bf16),
            pltpu.VMEM((SIDE, ROWS, E), f32),
            pltpu.VMEM((2, 4, 4, ROWS, HALF), bf16),
            pltpu.VMEM((2, 4, 4, ROWS, HALF), bf16),
            pltpu.VMEM((2, 4, ROWS, HALF), bf16),
            pltpu.VMEM((2, 4, ROWS, HALF), bf16),
            pltpu.VMEM((ROWS, E), f32),
            dma((2, 4)), dma((8,)), dma((SIDE,)),
            dma((2, 4)), dma((2, SIDE)), dma((2, SIDE)),
            dma((SIDE,)), dma((SIDE,)), dma((SIDE,)), dma((SIDE,)),
            dma((SIDE,)), dma((SIDE,)), dma((SIDE,)), dma((SIDE,)),
            dma((5,)), dma((5,)), dma((5, 8)), dma((5, 8)),
            dma((6, 4)), dma((6, 4)), dma((6, 4)), dma((6, 4)),
        ],
        compiler_params=pltpu.CompilerParams(
            collective_id=0, has_side_effects=True, vmem_limit_bytes=60 * 1024 * 1024
        ),
    )(images, texts, logit_scale)
    return loss, image_grad, text_grad


def solution(mesh):
    in_specs = (P(("img", "txt"), None), P(("txt", "img"), None), P())
    out_specs = (P(), P(("img", "txt"), None), P(("txt", "img"), None))
    return jax.shard_map(
        per_device, mesh=mesh, in_specs=in_specs, out_specs=out_specs, check_vma=False
    )
```

time: 1340 us -> 93 us (0.07)
  blocking collectives: 807 us -> 0 us
  waiting for transfers between devices: 483 us -> 0 us
  Pallas kernels: 0 us -> 87.4 us
  matrix products: 23.9 us -> 0 us
  between operations: 18.2 us -> 3.1 us
    psum x3 -> x0, blocking collectives: 490 us -> none  [the longest x1 297 us: per_device(): row_total = lax.psum(jnp.sum(jnp.exp(logits - row_peak[:, None]), 1), 'txt')]
    reduce_scatter x2 -> x0, waiting for transfers between devices: 332 us -> none  [the longest x1 332 us: per_device(): lax.psum_scatter(image_terms, 'txt', scatter_dimension=0, tiled=True)]
    pmax x2 -> x0, blocking collectives: 307 us -> none  [the longest x1 300 us: per_device(): row_peak = lax.pmax(jnp.max(logits, 1), 'txt')]
    all_gather x1 -> x0, waiting for transfers between devices: 150 us -> none  [per_device(): image_tile = lax.all_gather(images, 'txt', axis=0, tiled=True)]
    pallas_call x0 -> x1, Pallas kernels: none -> 87.4 us  [per_device(): pl.pallas_call(kernel, out_shape=(jax.ShapeDtypeStruct((1,), f32), jax.Sh...]
    dot_general x3 -> x0, matrix products: 23.9 us -> none  [the longest x1 9.41 us: per_device(): jnp.dot(weights, text_tile, preferred_element_type=jnp.float32)]
  transfers between devices with their start and end apart: 3 -> 0, of which waited for: 2 -> 0; matrix products, arithmetic and copies ran while one was open for 1% -> 0% of each run, Pallas kernels for 0% -> 0%
where the time goes in v1:
time: 93 us; the launch traced here: 92.9 us
  Pallas kernels  87.4 us (94%)
  between operations  3.1 us (3%)
  local copies, waits for them, and re-layouts  2.45 us (3%)
    pallas_call x1, Pallas kernels, per_device(): pl.pallas_call(kernel, out_shape=(jax.ShapeDtypeStruct((1,), f32), jax.Sh...  87.4 us
    unnamed x4, local copies, waits for them, and re-layouts  2.45 us

profile of v1, /device:TPU:1, one launch (start us, length us, event | category | flops | bytes accessed | tf_op | source)
XLA Modules:
  0.0 92.9 jit_solution(14961468276785209007)
XLA Ops:
  1.3 87.4 %shard_map.58 = (f32[1]{0:T(128)}, f32[56,1280]{1,0:T(8,128)}, f32[56,1280]{1,0:T(8,128)}) custom-call(bf16[56,1280]{1,0:T(8,128)(2,1)} %images_ref.1, bf16[56,1280]{1,0:T(8,128)(2,1)} %texts_ref.1, f32[1]{0:T(128)S(6)} %copy.9.scale_ref), custom_call_target="tpu_custom_call" | custom-call | tf_op jit(solution)/shard_map/pallas_call | solution.py:515
  89.3 0.0 copy-start
  89.3 1.7 %copy.11 = f32[56,1280]{1,0:T(8,128)} copy(f32[56,1280]{1,0:T(8,128)} %get-tuple-element.7) | data formatting | bytes 573440
  91.1 0.0 copy-done
  91.1 0.7 copy.12
Async XLA Ops:
  89.3 1.7 %copy-start = (f32[56,1280]{1,0:T(8,128)S(1)}, f32[56,1280]{1,0:T(8,128)}, u32[]{:S(2)}) copy-start(f32[56,1280]{1,0:T(8,128)} %get-tuple-element.8) | copy-start | bytes 860164

commit v2 on v0

v2 whole, which is shorter than its diff:
```python
import jax
import jax.numpy as jnp
from jax import lax
from jax.experimental import pallas as pl
from jax.experimental.pallas import tpu as pltpu
from jax.sharding import PartitionSpec as P

MESH = pl.DeviceIdType.MESH
ROWS = 56
PITCH = 64
SIDE = 16
TILE = SIDE * PITCH
CORE = 8 * PITCH
E = 1280
PAIRS = 14336
WIDE = 256
CHUNKS = E // WIDE
HALF = 640
FLOOR = -1e30
PIECES = (
    (0, 0, 256, 0),
    (1, 256, 256, 0),
    (0, 512, 256, 256),
    (1, 768, 256, 256),
    (0, 1024, 128, 512),
    (1, 1152, 128, 512),
)
NEAR = (1, 3, 2)


def device(x, y, z, c):
    return (lax.rem(x, 2) * 2 + c, (y * 8 + z) * 2 + lax.div(x, 2))


def kernel(
    images_ref, texts_ref, scale_ref,
    loss_ref, igrad_ref, tgrad_ref,
    ibuf, tbuf, ibig, tbig, tother, logits, prow, pcol, weights, wother, wturned,
    rsub, csum, cmax, dsum, frow, rmsg, cmsg, rstats, cstats, lmsg, lstats, pmsg, pstats,
    ipart, tpart, zout, zagg, zin, sout, sin, pout, pin, pkeep,
    own_sem, zsend, zrecv, isend, icross, tsend, ta0, ta1, tb0, tb1, tc, xsem,
    small_send, small_recv, zosend, zfirst, zlast, ssend, srecv, psend, precv,
):
    img = lax.axis_index("img")
    txt = lax.axis_index("txt")
    x_lo = lax.div(img, 2)
    c = lax.rem(img, 2)
    x_hi = lax.rem(txt, 2)
    x = x_hi * 2 + x_lo
    y = lax.div(txt, 16)
    z = lax.rem(lax.div(txt, 2), 8)
    oc = 1 - c
    islot = c * 8 + z
    tslot = x * 4 + y

    def x_at(d):
        return lax.rem(x + d, 4)

    def y_at(d):
        return lax.rem(y + d, 4)

    def z_at(d):
        return lax.rem(z + d + 8, 8)

    def row_peer(slot):
        return device(x, y, lax.rem(slot, 8), lax.div(slot, 8))

    def col_peer(slot):
        return device(lax.div(slot, 4), lax.rem(slot, 4), z, c)

    twin = device(x, y, z, oc)

    def copy(src, dst, send, recv, where):
        return pltpu.make_async_remote_copy(
            src_ref=src, dst_ref=dst, send_sem=send, recv_sem=recv,
            device_id=where, device_id_type=MESH,
        )

    def wait_on(ref, sem):
        copy(ref, ref, sem, sem, twin).wait_recv()

    barrier = pltpu.get_barrier_semaphore()

    def greet(k, carry):
        pl.semaphore_signal(barrier, inc=1, device_id=row_peer(lax.rem(islot + k, SIDE)), device_id_type=MESH)
        pl.semaphore_signal(barrier, inc=1, device_id=col_peer(lax.rem(tslot + k, SIDE)), device_id_type=MESH)
        return carry

    lax.fori_loop(1, SIDE, greet, 0)
    own_image = pltpu.make_async_copy(images_ref, ibuf.at[islot], own_sem.at[0])
    own_text = pltpu.make_async_copy(texts_ref, tbuf.at[tslot], own_sem.at[1])
    own_image.start()
    own_text.start()
    ibig[...] = jnp.zeros_like(ibig)
    tbig[...] = jnp.zeros_like(tbig)
    own_image.wait()
    own_text.wait()
    pl.semaphore_wait(barrier, 2 * (SIDE - 1))

    def half_of(buf, slot, half):
        return buf.at[slot, :, pl.ds(half * HALF, HALF)]

    def z_copy(owner, way, half):
        ref = half_of(ibuf, c * 8 + owner, half)
        return copy(ref, ref, zsend.at[0], zrecv.at[half * 8 + owner], device(x, y, z_at(1 if way == 0 else -1), c))

    def z_wait(owner, half):
        wait_on(half_of(ibuf, c * 8 + owner, half), zrecv.at[half * 8 + owner])

    def cross_copy(owner):
        ref = ibuf.at[c * 8 + owner]
        return copy(ref, ref, isend.at[0], icross.at[owner], twin)

    def t_copy(slot, half, sem, where):
        ref = half_of(tbuf, slot, half)
        return copy(ref, ref, tsend.at[0], sem, where)

    def place(buf, big, slot):
        big[pl.ds(pl.multiple_of(slot * PITCH, PITCH), ROWS), :] = buf[slot]

    z_copy(z, 0, 0).start()
    z_copy(z, 1, 0).start()
    for d in NEAR:
        t_copy(tslot, 0, ta0.at[x], device(x_at(d), y, z, c)).start()
        t_copy(tslot, 1, ta1.at[y], device(x, y_at(d), z, c)).start()
    z_copy(z, 0, 1).start()
    z_copy(z, 1, 1).start()
    for d in NEAR:
        t_copy(tslot, 1, tb0.at[x], device(x_at(d), y, z, c)).start()
        t_copy(tslot, 0, tb1.at[0], device(x, y_at(d), z, c)).start()
    cross_copy(z).start()
    place(ibuf, ibig, islot)
    place(tbuf, tbig, tslot)
    weights[...] = jnp.zeros_like(weights)
    rsub[...] = jnp.zeros_like(rsub)

    def z_step(step, half):
        left = z_at(-1 - step)
        right = z_at(1 + step)
        z_wait(left, half)
        if step < 2:
            z_copy(left, 0, half).start()
        else:
            @pl.when(c == 0)
            def _():
                z_copy(left, 0, half).start()
        z_wait(right, half)
        if step < 2:
            z_copy(right, 1, half).start()
        else:
            @pl.when(c == 1)
            def _():
                z_copy(right, 1, half).start()
        if half == 1:
            cross_copy(left).start()
            cross_copy(right).start()
            place(ibuf, ibig, c * 8 + left)
            place(ibuf, ibig, c * 8 + right)

    def t_step(d):
        slot0 = x_at(d) * 4 + y
        slot1 = x * 4 + y_at(d)
        wait_on(half_of(tbuf, slot0, 0), ta0.at[x_at(d)])
        for e in NEAR:
            t_copy(slot0, 0, tc.at[x_at(d)], device(x, y_at(e), z, c)).start()
        wait_on(half_of(tbuf, slot1, 1), ta1.at[y_at(d)])
        for e in NEAR:
            t_copy(slot1, 1, tc.at[x], device(x_at(e), y, z, c)).start()

    z_step(0, 0)
    t_step(1)
    z_step(0, 1)
    t_step(3)
    z_step(1, 0)
    t_step(2)
    z_step(1, 1)
    z_step(2, 0)
    z_step(2, 1)
    far = z_at(4)
    z_wait(far, 0)
    z_wait(far, 1)
    cross_copy(far).start()
    place(ibuf, ibig, c * 8 + far)
    wait_on(tbuf.at[pl.ds(0, 3), :, pl.ds(0, HALF)], tb1.at[0])
    for d in NEAR:
        place(tbuf, tbig, x * 4 + y_at(d))

    def other_image(k, carry):
        wait_on(ibuf.at[oc * 8 + k], icross.at[k])
        place(ibuf, ibig, oc * 8 + k)
        return carry

    lax.fori_loop(0, 8, other_image, 0)

    scale = scale_ref[0]

    def score(tile):
        cols = pl.ds(pl.multiple_of(tile * WIDE, WIDE), WIDE)
        part = lax.dot_general(
            ibig[...], tbig[cols, :], (((1,), (1,)), ((), ())), preferred_element_type=jnp.float32
        )
        pad = lax.bitwise_and(lax.broadcasted_iota(jnp.int32, (1, WIDE), 1), PITCH - 1) >= ROWS
        logits[:, cols] = jnp.where(pad, FLOOR, part * scale)

    score(x)
    for d in NEAR:
        tile = x_at(d)
        wait_on(half_of(tbuf, tile * 4 + y, 1), tb0.at[tile])
        wait_on(tbuf.at[pl.ds(0, 3)], tc.at[tile])
        for e in range(4):
            place(tbuf, tbig, tile * 4 + e)
        score(tile)
    text_swap = copy(tbig, tother, xsem.at[0], xsem.at[1], twin)
    text_swap.start()

    def rows_of(k):
        return pl.ds(pl.multiple_of(k * PITCH, PITCH), ROWS)

    cmax[...] = jnp.full_like(cmax, FLOOR)

    def col_max(k, carry):
        cmax[...] = jnp.maximum(cmax[...], jnp.max(logits[rows_of(k), :].reshape(7, 8, TILE), 0))
        return carry

    lax.fori_loop(0, SIDE, col_max, 0)
    col_top = jnp.max(cmax[...], 0, keepdims=True)
    csum[...] = jnp.zeros_like(csum)

    def exponentials(k, carry):
        part = logits[rows_of(k), :]
        top = jnp.max(part, 1, keepdims=True)
        by_row = jnp.exp(part - top)
        by_col = jnp.exp(part - col_top)
        prow[rows_of(k), :] = by_row
        pcol[rows_of(k), :] = by_col
        total = jnp.sum(by_row, 1, keepdims=True)
        first = lax.broadcasted_iota(jnp.int32, (ROWS, 128), 1) == 0
        rsub[rows_of(k), :] = jnp.where(first, top, total)
        csum[...] += jnp.sum(by_col.reshape(7, 8, TILE), 0)
        return carry

    lax.fori_loop(0, SIDE, exponentials, 0)

    row_stats = jnp.transpose(rsub[...], (1, 0))
    col_total_here = jnp.sum(csum[...], 0, keepdims=True)
    for k in range(4):
        part = slice(k * WIDE, (k + 1) * WIDE)
        rmsg[k:k + 1, :] = row_stats[0:1, part]
        rmsg[4 + k:5 + k, :] = row_stats[1:2, part]
        cmsg[k:k + 1, :] = col_top[:, part]
        cmsg[4 + k:5 + k, :] = col_total_here[:, part]

    def spread(msg, stats, which, mine, peer_of):
        stats[mine] = msg[...]

        def send(k, carry):
            copy(msg, stats.at[mine], small_send.at[which], small_recv.at[which], peer_of(lax.rem(mine + k, SIDE))).start()
            return carry

        lax.fori_loop(1, SIDE, send, 0)

    def collect(stats, which):
        wait_on(stats.at[pl.ds(0, SIDE - 1)], small_recv.at[which])

    spread(rmsg, rstats, 0, islot, row_peer)
    spread(cmsg, cstats, 1, tslot, col_peer)

    def diagonal_slot(k):
        row_block = (x_lo * 2 + lax.div(k, 8)) * 64 + (y * 8 + lax.rem(k, 8)) * 2 + x_hi
        here = jnp.logical_and(lax.rem(row_block, 2) == c, lax.rem(lax.div(row_block, 8), 8) == z)
        slot = (lax.rem(lax.div(row_block, 4), 2) * 2 + lax.rem(lax.div(row_block, 2), 2)) * 4 + lax.div(row_block, 64)
        return here, slot

    def pair_mask(slot):
        row = lax.broadcasted_iota(jnp.int32, (ROWS, 128), 0)
        lane = lax.broadcasted_iota(jnp.int32, (ROWS, 128), 1)
        return lane == row + lax.rem(slot, 2) * PITCH

    def pair_cols(slot):
        return pl.ds(pl.multiple_of(lax.div(slot, 2) * 128, 128), 128)

    dsum[...] = jnp.zeros_like(dsum)

    def diagonal_logits(k, carry):
        here, slot = diagonal_slot(k)

        @pl.when(here)
        def _():
            picked = jnp.where(pair_mask(slot), logits[rows_of(k), pair_cols(slot)], 0.0)
            dsum[...] += jnp.sum(picked.reshape(7, 8, 128), 0)

        return carry

    lax.fori_loop(0, SIDE, diagonal_logits, 0)
    collect(rstats, 0)

    def combine(stats, mine):
        peaks = stats[:, 0:4, :]
        totals = stats[:, 4:8, :]
        peak = jnp.max(peaks, 0)
        total = jnp.sum(totals * jnp.exp(peaks - peak[None]), 0)
        factor = 0.5 * jnp.exp(mine[0:4, :] - peak) / total
        return peak + jnp.log(total), factor

    def line(v):
        return jnp.concatenate([v[k:k + 1, :] for k in range(4)], 1)

    row_lse, row_factor = combine(rstats, rmsg)
    frow[...] = jnp.transpose(jnp.broadcast_to(line(row_factor), (128, TILE)), (1, 0))
    collect(cstats, 1)
    col_lse, col_factor = combine(cstats, cmsg)
    csum[0:1, :] = line(col_factor)

    def weigh(k, carry):
        factor = frow[rows_of(k), :][:, 0:1]
        w = factor * prow[rows_of(k), :] + csum[0:1, :] * pcol[rows_of(k), :]
        weights[rows_of(k), :] = w.astype(jnp.bfloat16)
        here, slot = diagonal_slot(k)

        @pl.when(here)
        def _():
            cols = pair_cols(slot)
            v = frow[rows_of(k), :] * prow[rows_of(k), cols] + csum[0:1, cols] * pcol[rows_of(k), cols]
            v = v - jnp.where(pair_mask(slot), 1.0, 0.0)
            weights[rows_of(k), cols] = v.astype(jnp.bfloat16)

        return carry

    lax.fori_loop(oc * 8, oc * 8 + 8, weigh, 0)
    weight_swap = copy(
        weights.at[pl.ds(pl.multiple_of(oc * CORE, CORE), CORE), :], wother, xsem.at[2], xsem.at[3], twin
    )
    weight_swap.start()
    lax.fori_loop(c * 8, c * 8 + 8, weigh, 0)

    index = lax.broadcasted_iota(jnp.int32, (4, WIDE), 0) * WIDE + lax.broadcasted_iota(jnp.int32, (4, WIDE), 1)
    slot_of = lax.shift_right_logical(index, 6)
    valid = lax.bitwise_and(index, PITCH - 1) < ROWS
    terms = jnp.where(valid & (slot_of == islot), row_lse, 0.0) + jnp.where(valid & (slot_of == tslot), col_lse, 0.0)
    term = jnp.sum(jnp.sum(terms, 0, keepdims=True), 1, keepdims=True)
    diagonal = jnp.sum(jnp.sum(dsum[...], 0, keepdims=True), 1, keepdims=True)
    lmsg[...] = jnp.broadcast_to(term - 2.0 * diagonal, (8, 128))
    spread(lmsg, lstats, 2, islot, row_peer)

    for k in range(TILE // 128):
        wturned[:, k * 128:(k + 1) * 128] = jnp.transpose(weights[k * 128:(k + 1) * 128, :], (1, 0))

    def first_peer(axis, f):
        return device(x, f, z, c) if axis == 0 else device(f, y, z, c)

    def second_peer(axis, s):
        return device(s, y, z, c) if axis == 0 else device(x, s, z, c)

    def slab_copy(p, d):
        axis, _, width, at = PIECES[p]
        me = y if axis == 0 else x
        there = lax.rem(me + d, 4)
        cols = pl.ds(at, width)
        return copy(
            sout.at[axis, there, :, :, cols], sin.at[axis, d - 1, :, :, cols],
            ssend.at[0], srecv.at[p], first_peer(axis, there),
        )

    def text_terms(n):
        low = n * WIDE
        tpart[:, low:low + WIDE] = jnp.dot(wturned[...], ibig[:, low:low + WIDE], preferred_element_type=jnp.float32)
        for p, (axis, col, width, at) in enumerate(PIECES):
            if col // WIDE != n:
                continue
            for m in range(SIDE):
                first, second = (m % 4, m // 4) if axis == 0 else (m // 4, m % 4)
                piece = tpart[m * PITCH:m * PITCH + ROWS, col:col + width]
                sout[axis, first, second, :, at:at + width] = piece.astype(jnp.bfloat16)
            for d in (2, 1, 3):
                slab_copy(p, d).start()

    def keep_copy(p, d):
        axis, _, width, at = PIECES[p]
        me = x if axis == 0 else y
        there = lax.rem(me + d, 4)
        cols = pl.ds(at, width)
        return copy(
            pout.at[axis, there, :, cols], pin.at[axis, d - 1, :, cols],
            psend.at[0], precv.at[p], second_peer(axis, there),
        )

    def text_second(p):
        axis, col, width, at = PIECES[p]
        wait_on(sin.at[axis, pl.ds(0, 3), :, :, pl.ds(at, width)], srecv.at[p])
        me = x if axis == 0 else y
        for d in (2, 1, 3, 0):
            s = lax.rem(me + d, 4)
            m = s * 4 + y if axis == 0 else x * 4 + s
            total = tpart[rows_of(m), col:col + width]
            for e in range(3):
                total = total + sin[axis, e, s, :, at:at + width].astype(jnp.float32)
            if d == 0:
                pkeep[:, col:col + width] = total
            else:
                pout[axis, s, :, at:at + width] = total.astype(jnp.bfloat16)
                keep_copy(p, d).start()

    def text_last(p):
        axis, col, width, at = PIECES[p]
        wait_on(pin.at[axis, pl.ds(0, 3), :, pl.ds(at, width)], precv.at[p])
        total = pkeep[:, col:col + width]
        for d in range(3):
            total = total + pin[axis, d, :, at:at + width].astype(jnp.float32)
        tgrad_ref[:, col:col + width] = total

    def image_send(n, src, slot, low, width, sem, d):
        return copy(
            src, zin.at[slot, :, pl.ds(low, width)], zosend.at[0], sem.at[n], device(x, y, z_at(d), c)
        )

    def image_terms(n):
        low = n * WIDE
        cols = pl.ds(low, WIDE)
        mine = pl.ds(pl.multiple_of(c * CORE, CORE), CORE)
        part = jnp.dot(weights[mine, :], tbig[:, cols], preferred_element_type=jnp.float32)
        ipart[:, cols] = part + jnp.dot(wother[...], tother[:, cols], preferred_element_type=jnp.float32)
        for d in (3, -3, 4, 1, -1):
            zout[z_at(d), :, cols] = ipart[rows_of(z_at(d)), cols].astype(jnp.bfloat16)
        image_send(n, zout.at[z_at(4), :, pl.ds(low, 128)], 2, low, 128, zfirst, 2).start()
        image_send(n, zout.at[z_at(4), :, pl.ds(low + 128, 128)], 2, low + 128, 128, zfirst, -2).start()
        image_send(n, zout.at[z_at(3), :, cols], 0, low, WIDE, zfirst, 1).start()
        image_send(n, zout.at[z_at(-3), :, cols], 1, low, WIDE, zfirst, -1).start()
        image_send(n, zout.at[z_at(1), :, cols], 3, low, WIDE, zlast, 1).start()
        image_send(n, zout.at[z_at(-1), :, cols], 4, low, WIDE, zlast, -1).start()

    def image_second(n):
        low = n * WIDE
        cols = pl.ds(low, WIDE)
        wait_on(zin.at[pl.ds(0, 3), :, cols], zfirst.at[n])
        for way in range(2):
            d = 2 if way == 0 else -2
            total = ipart[rows_of(z_at(d)), cols] + zin[way, :, cols].astype(jnp.float32)
            edge = low + way * 128
            side = total[:, way * 128:way * 128 + 128] + zin[2, :, edge:edge + 128].astype(jnp.float32)
            rest = low + 128 - way * 128
            zagg[way, :, edge:edge + 128] = side.astype(jnp.bfloat16)
            zagg[way, :, rest:rest + 128] = total[:, 128 - way * 128:256 - way * 128].astype(jnp.bfloat16)
            image_send(n, zagg.at[way, :, cols], 5 + way, low, WIDE, zlast, d).start()

    def image_last(n):
        cols = pl.ds(n * WIDE, WIDE)
        wait_on(zin.at[pl.ds(3, 4), :, cols], zlast.at[n])
        total = ipart[rows_of(z), cols]
        for k in range(3, 7):
            total = total + zin[k, :, cols].astype(jnp.float32)
        igrad_ref[:, cols] = total

    text_terms(0)
    text_swap.wait()
    weight_swap.wait()
    image_terms(0)
    text_terms(1)
    image_terms(1)
    image_second(0)
    text_terms(2)
    image_terms(2)
    image_second(1)
    text_second(0)
    text_terms(3)
    image_terms(3)
    image_second(2)
    text_second(1)
    text_terms(4)
    image_terms(4)
    image_second(3)
    text_second(2)
    collect(lstats, 2)
    pmsg[...] = jnp.sum(lstats[...], 0)
    spread(pmsg, pstats, 3, tslot, col_peer)
    image_second(4)
    text_second(3)
    text_second(4)
    text_second(5)
    for n in range(CHUNKS):
        image_last(n)
        text_last(n)
    text_last(5)
    collect(pstats, 3)
    loss_ref[...] = (jnp.sum(pstats[...], 0) / (2.0 * PAIRS))[0:1, 0:1]

    wait_on(ibuf.at[pl.ds(0, 7)], zsend.at[0])
    wait_on(ibuf.at[pl.ds(0, 8)], isend.at[0])
    wait_on(tbuf.at[pl.ds(0, 15)], tsend.at[0])
    wait_on(rstats.at[pl.ds(0, SIDE - 1)], small_send.at[0])
    wait_on(cstats.at[pl.ds(0, SIDE - 1)], small_send.at[1])
    wait_on(lstats.at[pl.ds(0, SIDE - 1)], small_send.at[2])
    wait_on(pstats.at[pl.ds(0, SIDE - 1)], small_send.at[3])
    wait_on(zin, zosend.at[0])
    wait_on(sout.at[:, pl.ds(0, 3)], ssend.at[0])
    wait_on(pout.at[:, pl.ds(0, 3)], psend.at[0])


def per_device(images, texts, logit_scale):
    f32, bf16 = jnp.float32, jnp.bfloat16
    dma = pltpu.SemaphoreType.DMA
    vmem = pl.BlockSpec(memory_space=pltpu.VMEM)
    smem = pl.BlockSpec(memory_space=pltpu.SMEM)
    hbm = pl.BlockSpec(memory_space=pl.ANY)
    loss, image_grad, text_grad = pl.pallas_call(
        kernel,
        out_shape=(
            jax.ShapeDtypeStruct((1, 1), f32),
            jax.ShapeDtypeStruct((ROWS, E), f32),
            jax.ShapeDtypeStruct((ROWS, E), f32),
        ),
        in_specs=[hbm, hbm, smem],
        out_specs=(vmem, vmem, vmem),
        scratch_shapes=[
            pltpu.VMEM((SIDE, ROWS, E), bf16),
            pltpu.VMEM((SIDE, ROWS, E), bf16),
            pltpu.VMEM((TILE, E), bf16),
            pltpu.VMEM((TILE, E), bf16),
            pltpu.VMEM((TILE, E), bf16),
            pltpu.VMEM((TILE, TILE), f32),
            pltpu.VMEM((TILE, TILE), f32),
            pltpu.VMEM((TILE, TILE), f32),
            pltpu.VMEM((TILE, TILE), bf16),
            pltpu.VMEM((CORE, TILE), bf16),
            pltpu.VMEM((TILE, TILE), bf16),
            pltpu.VMEM((TILE, 128), f32),
            pltpu.VMEM((8, TILE), f32),
            pltpu.VMEM((8, TILE), f32),
            pltpu.VMEM((8, 128), f32),
            pltpu.VMEM((TILE, 128), f32),
            pltpu.VMEM((8, WIDE), f32),
            pltpu.VMEM((8, WIDE), f32),
            pltpu.VMEM((SIDE, 8, WIDE), f32),
            pltpu.VMEM((SIDE, 8, WIDE), f32),
            pltpu.VMEM((8, 128), f32),
            pltpu.VMEM((SIDE, 8, 128), f32),
            pltpu.VMEM((8, 128), f32),
            pltpu.VMEM((SIDE, 8, 128), f32),
            pltpu.VMEM((CORE, E), f32),
            pltpu.VMEM((TILE, E), f32),
            pltpu.VMEM((8, ROWS, E), bf16),
            pltpu.VMEM((2, ROWS, E), bf16),
            pltpu.VMEM((7, ROWS, E), bf16),
            pltpu.VMEM((2, 4, 4, ROWS, HALF), bf16),
            pltpu.VMEM((2, 3, 4, ROWS, HALF), bf16),
            pltpu.VMEM((2, 4, ROWS, HALF), bf16),
            pltpu.VMEM((2, 3, ROWS, HALF), bf16),
            pltpu.VMEM((ROWS, E), f32),
            dma((2,)), dma((1,)), dma((16,)), dma((1,)), dma((8,)),
            dma((1,)), dma((4,)), dma((4,)), dma((4,)), dma((1,)), dma((4,)), dma((4,)),
            dma((4,)), dma((4,)), dma((1,)), dma((5,)), dma((5,)),
            dma((1,)), dma((6,)), dma((1,)), dma((6,)),
        ],
        compiler_params=pltpu.CompilerParams(
            collective_id=0, has_side_effects=True, vmem_limit_bytes=60 * 1024 * 1024
        ),
    )(images, texts, logit_scale)
    return loss.reshape(1), image_grad, text_grad


def solution(mesh):
    in_specs = (P(("img", "txt"), None), P(("txt", "img"), None), P())
    out_specs = (P(), P(("img", "txt"), None), P(("txt", "img"), None))
    return jax.shard_map(
        per_device, mesh=mesh, in_specs=in_specs, out_specs=out_specs, check_vma=False
    )
```

time: 1340 us -> 77.9 us (0.06)
  blocking collectives: 807 us -> 0 us
  waiting for transfers between devices: 483 us -> 0 us
  Pallas kernels: 0 us -> 72.2 us
  matrix products: 23.9 us -> 0 us
  between operations: 18.2 us -> 3.1 us
    psum x3 -> x0, blocking collectives: 490 us -> none  [the longest x1 297 us: per_device(): row_total = lax.psum(jnp.sum(jnp.exp(logits - row_peak[:, None]), 1), 'txt')]
    reduce_scatter x2 -> x0, waiting for transfers between devices: 332 us -> none  [the longest x1 332 us: per_device(): lax.psum_scatter(image_terms, 'txt', scatter_dimension=0, tiled=True)]
    pmax x2 -> x0, blocking collectives: 307 us -> none  [the longest x1 300 us: per_device(): row_peak = lax.pmax(jnp.max(logits, 1), 'txt')]
    all_gather x1 -> x0, waiting for transfers between devices: 150 us -> none  [per_device(): image_tile = lax.all_gather(images, 'txt', axis=0, tiled=True)]
    pallas_call x0 -> x1, Pallas kernels: none -> 72.2 us  [per_device(): pl.pallas_call(kernel, out_shape=(jax.ShapeDtypeStruct((1, 1), f32), jax....]
    dot_general x3 -> x0, matrix products: 23.9 us -> none  [the longest x1 9.41 us: per_device(): jnp.dot(weights, text_tile, preferred_element_type=jnp.float32)]
  transfers between devices with their start and end apart: 3 -> 0, of which waited for: 2 -> 0; matrix products, arithmetic and copies ran while one was open for 1% -> 0% of each run, Pallas kernels for 0% -> 0%
where the time goes in v2:
time: 77.9 us; the launch traced here: 77.8 us
  Pallas kernels  72.2 us (93%)
  between operations  3.1 us (4%)
  local copies, waits for them, and re-layouts  2.45 us (3%)
    pallas_call x1, Pallas kernels, per_device(): pl.pallas_call(kernel, out_shape=(jax.ShapeDtypeStruct((1, 1), f32), jax....  72.2 us
    unnamed x4, local copies, waits for them, and re-layouts  2.45 us

profile of v2, /device:TPU:1, one launch (start us, length us, event | category | flops | bytes accessed | tf_op | source)
XLA Modules:
  0.0 77.8 jit_solution(1133957543412851444)
XLA Ops:
  1.3 72.2 %shard_map.58 = (f32[1,1]{1,0:T(1,128)}, f32[56,1280]{1,0:T(8,128)}, f32[56,1280]{1,0:T(8,128)}) custom-call(bf16[56,1280]{1,0:T(8,128)(2,1)} %images_ref.1, bf16[56,1280]{1,0:T(8,128)(2,1)} %texts_ref.1, f32[1]{0:T(128)S(6)} %copy.9.scale_ref), custom_call_target="tpu_custom_call" | custom-call | tf_op jit(solution)/shard_map/pallas_call | solution.py:504
  74.2 0.0 copy-start
  74.2 1.7 %copy.11 = f32[56,1280]{1,0:T(8,128)} copy(f32[56,1280]{1,0:T(8,128)} %get-tuple-element.13) | data formatting | bytes 573440
  75.9 0.0 copy-done
  75.9 0.7 copy.12
Async XLA Ops:
  74.2 1.7 %copy-start = (f32[56,1280]{1,0:T(8,128)S(1)}, f32[56,1280]{1,0:T(8,128)}, u32[]{:S(2)}) copy-start(f32[56,1280]{1,0:T(8,128)} %get-tuple-element.14) | copy-start | bytes 860164

commit v3 on v2

--- a/solution.py
+++ b/solution.py
@@ -36,9 +36,9 @@
     images_ref, texts_ref, scale_ref,
     loss_ref, igrad_ref, tgrad_ref,
     ibuf, tbuf, ibig, tbig, tother, logits, prow, pcol, weights, wother, wturned,
-    rsub, csum, cmax, dsum, frow, rmsg, cmsg, rstats, cstats, lmsg, lstats, pmsg, pstats,
+    rsub, csum, cmax, cpeak, cfac, dsum, frow, rmsg, cmsg, rstats, cstats, lmsg, lstats, pmsg, pstats,
     ipart, tpart, zout, zagg, zin, sout, sin, pout, pin, pkeep,
-    own_sem, zsend, zrecv, isend, icross, tsend, ta0, ta1, tb0, tb1, tc, xsem,
+    own_sem, zsend, zrecv, isend, icross, tsend, tfirst, tplus, tminus, tfar, xsem,
     small_send, small_recv, zosend, zfirst, zlast, ssend, srecv, psend, precv,
 ):
     img = lax.axis_index("img")
@@ -111,23 +111,62 @@
         ref = ibuf.at[c * 8 + owner]
         return copy(ref, ref, isend.at[0], icross.at[owner], twin)
 
-    def t_copy(slot, half, sem, where):
-        ref = half_of(tbuf, slot, half)
-        return copy(ref, ref, tsend.at[0], sem, where)
+    def t_slot(half, u, v):
+        return u * 4 + v if half == 0 else v * 4 + u
+
+    def t_here(half):
+        return (x, y) if half == 0 else (y, x)
+
+    def t_device(half, u, v):
+        return device(u, v, z, c) if half == 0 else device(v, u, z, c)
+
+    def t_send(half, u, v, sem, to_u, to_v):
+        ref = half_of(tbuf, t_slot(half, u, v), half)
+        copy(ref, ref, tsend.at[0], sem.at[half * 4 + u], t_device(half, to_u, to_v)).start()
+
+    def t_wait(half, u, v, sem):
+        wait_on(half_of(tbuf, t_slot(half, u, v), half), sem.at[half * 4 + u])
+
+    def t_first(half):
+        u, v = t_here(half)
+        for d in NEAR:
+            t_send(half, u, v, tfirst, lax.rem(u + d, 4), v)
+
+    def t_second(half, d):
+        u, v = t_here(half)
+        there = lax.rem(u + d, 4)
+        if d:
+            t_wait(half, there, v, tfirst)
+        t_send(half, there, v, tplus, u, lax.rem(v + 1, 4))
+        t_send(half, there, v, tminus, u, lax.rem(v + 3, 4))
+
+    def t_pass(half, d):
+        u, v = t_here(half)
+        there = lax.rem(u + d, 4)
+        before = lax.rem(v + 3, 4)
+        after = lax.rem(v + 1, 4)
+        t_wait(half, there, before, tplus)
+        if d < 2:
+            t_send(half, there, before, tfar, u, after)
+        t_wait(half, there, after, tminus)
+        if d >= 2:
+            t_send(half, there, after, tfar, u, before)
+
+    def t_last(half, d):
+        u, v = t_here(half)
+        t_wait(half, lax.rem(u + d, 4), lax.rem(v + 2, 4), tfar)
 
     def place(buf, big, slot):
         big[pl.ds(pl.multiple_of(slot * PITCH, PITCH), ROWS), :] = buf[slot]
 
+    t_first(0)
+    t_first(1)
     z_copy(z, 0, 0).start()
     z_copy(z, 1, 0).start()
-    for d in NEAR:
-        t_copy(tslot, 0, ta0.at[x], device(x_at(d), y, z, c)).start()
-        t_copy(tslot, 1, ta1.at[y], device(x, y_at(d), z, c)).start()
+    t_second(0, 0)
+    t_second(1, 0)
     z_copy(z, 0, 1).start()
     z_copy(z, 1, 1).start()
-    for d in NEAR:
-        t_copy(tslot, 1, tb0.at[x], device(x_at(d), y, z, c)).start()
-        t_copy(tslot, 0, tb1.at[0], device(x, y_at(d), z, c)).start()
     cross_copy(z).start()
     place(ibuf, ibig, islot)
     place(tbuf, tbig, tslot)
@@ -157,34 +196,28 @@
             place(ibuf, ibig, c * 8 + left)
             place(ibuf, ibig, c * 8 + right)
 
-    def t_step(d):
-        slot0 = x_at(d) * 4 + y
-        slot1 = x * 4 + y_at(d)
-        wait_on(half_of(tbuf, slot0, 0), ta0.at[x_at(d)])
-        for e in NEAR:
-            t_copy(slot0, 0, tc.at[x_at(d)], device(x, y_at(e), z, c)).start()
-        wait_on(half_of(tbuf, slot1, 1), ta1.at[y_at(d)])
-        for e in NEAR:
-            t_copy(slot1, 1, tc.at[x], device(x_at(e), y, z, c)).start()
+    def t_both(what, d):
+        what(0, d)
+        what(1, d)
 
     z_step(0, 0)
-    t_step(1)
+    t_both(t_second, 1)
     z_step(0, 1)
-    t_step(3)
+    t_both(t_second, 3)
+    t_both(t_pass, 0)
     z_step(1, 0)
-    t_step(2)
+    t_both(t_second, 2)
+    t_both(t_pass, 1)
     z_step(1, 1)
+    t_both(t_pass, 3)
     z_step(2, 0)
+    t_both(t_pass, 2)
     z_step(2, 1)
     far = z_at(4)
     z_wait(far, 0)
     z_wait(far, 1)
     cross_copy(far).start()
     place(ibuf, ibig, c * 8 + far)
-    wait_on(tbuf.at[pl.ds(0, 3), :, pl.ds(0, HALF)], tb1.at[0])
-    for d in NEAR:
-        place(tbuf, tbig, x * 4 + y_at(d))
-
     def other_image(k, carry):
         wait_on(ibuf.at[oc * 8 + k], icross.at[k])
         place(ibuf, ibig, oc * 8 + k)
@@ -202,53 +235,73 @@
         pad = lax.bitwise_and(lax.broadcasted_iota(jnp.int32, (1, WIDE), 1), PITCH - 1) >= ROWS
         logits[:, cols] = jnp.where(pad, FLOOR, part * scale)
 
-    score(x)
-    for d in NEAR:
-        tile = x_at(d)
-        wait_on(half_of(tbuf, tile * 4 + y, 1), tb0.at[tile])
-        wait_on(tbuf.at[pl.ds(0, 3)], tc.at[tile])
-        for e in range(4):
-            place(tbuf, tbig, tile * 4 + e)
-        score(tile)
-    text_swap = copy(tbig, tother, xsem.at[0], xsem.at[1], twin)
-    text_swap.start()
-
     def rows_of(k):
         return pl.ds(pl.multiple_of(k * PITCH, PITCH), ROWS)
 
-    cmax[...] = jnp.full_like(cmax, FLOOR)
-
-    def col_max(k, carry):
-        cmax[...] = jnp.maximum(cmax[...], jnp.max(logits[rows_of(k), :].reshape(7, 8, TILE), 0))
-        return carry
-
-    lax.fori_loop(0, SIDE, col_max, 0)
-    col_top = jnp.max(cmax[...], 0, keepdims=True)
-    csum[...] = jnp.zeros_like(csum)
-
-    def exponentials(k, carry):
-        part = logits[rows_of(k), :]
-        top = jnp.max(part, 1, keepdims=True)
-        by_row = jnp.exp(part - top)
-        by_col = jnp.exp(part - col_top)
-        prow[rows_of(k), :] = by_row
-        pcol[rows_of(k), :] = by_col
-        total = jnp.sum(by_row, 1, keepdims=True)
-        first = lax.broadcasted_iota(jnp.int32, (ROWS, 128), 1) == 0
-        rsub[rows_of(k), :] = jnp.where(first, top, total)
-        csum[...] += jnp.sum(by_col.reshape(7, 8, TILE), 0)
-        return carry
-
-    lax.fori_loop(0, SIDE, exponentials, 0)
+    def tile_cols(d):
+        return pl.ds(pl.multiple_of(x_at(d) * WIDE, WIDE), WIDE)
+
+    def swap_texts(d):
+        rows = tile_cols(d)
+        return copy(tbig.at[rows, :], tother.at[rows, :], xsem.at[0], xsem.at[1], twin)
+
+    def exponentials(d):
+        cols = tile_cols(d)
+        cmax[...] = jnp.full_like(cmax, FLOOR)
+
+        def col_max(k, carry):
+            cmax[...] = jnp.maximum(cmax[...], jnp.max(logits[rows_of(k), cols].reshape(7, 8, WIDE), 0))
+            return carry
+
+        lax.fori_loop(0, SIDE, col_max, 0)
+        top = jnp.max(cmax[...], 0, keepdims=True)
+        cpeak[0:1, cols] = top
+        csum[:, cols] = jnp.zeros((8, WIDE), jnp.float32)
+
+        def one(k, carry):
+            part = logits[rows_of(k), cols]
+            peak = jnp.max(part, 1, keepdims=True)
+            by_row = jnp.exp(part - peak)
+            by_col = jnp.exp(part - top)
+            prow[rows_of(k), cols] = by_row
+            pcol[rows_of(k), cols] = by_col
+            total = jnp.sum(by_row, 1, keepdims=True)
+            at = lax.broadcasted_iota(jnp.int32, (ROWS, 128), 1)
+            rsub[rows_of(k), :] = jnp.where(at == 2 * d, peak, jnp.where(at == 2 * d + 1, total, rsub[rows_of(k), :]))
+            csum[:, cols] += jnp.sum(by_col.reshape(7, 8, WIDE), 0)
+            return carry
+
+        lax.fori_loop(0, SIDE, one, 0)
+
+    for d in (0, 1, 3, 2):
+        t_last(0, d)
+        if d == 2:
+            for e in range(4):
+                t_last(1, e)
+        for e in range(1 if d == 0 else 0, 4):
+            place(tbuf, tbig, x_at(d) * 4 + y_at(e))
+        swap_texts(d).start()
+        score(x_at(d))
+        exponentials(d)
 
     row_stats = jnp.transpose(rsub[...], (1, 0))
-    col_total_here = jnp.sum(csum[...], 0, keepdims=True)
-    for k in range(4):
-        part = slice(k * WIDE, (k + 1) * WIDE)
-        rmsg[k:k + 1, :] = row_stats[0:1, part]
-        rmsg[4 + k:5 + k, :] = row_stats[1:2, part]
-        cmsg[k:k + 1, :] = col_top[:, part]
-        cmsg[4 + k:5 + k, :] = col_total_here[:, part]
+
+    def fold(v):
+        return jnp.concatenate([v[:, k * WIDE:(k + 1) * WIDE] for k in range(4)], 0)
+
+    def line(v):
+        return jnp.concatenate([v[k:k + 1, :] for k in range(4)], 1)
+
+    tile_peaks = [fold(row_stats[2 * d:2 * d + 1, :]) for d in range(4)]
+    tile_totals = [fold(row_stats[2 * d + 1:2 * d + 2, :]) for d in range(4)]
+    row_top = jnp.maximum(jnp.maximum(tile_peaks[0], tile_peaks[1]), jnp.maximum(tile_peaks[2], tile_peaks[3]))
+    row_total = jnp.zeros_like(row_top)
+    for d in range(4):
+        row_total = row_total + tile_totals[d] * jnp.exp(tile_peaks[d] - row_top)
+    rmsg[0:4, :] = row_top
+    rmsg[4:8, :] = row_total
+    cmsg[0:4, :] = fold(cpeak[0:1, :])
+    cmsg[4:8, :] = fold(jnp.sum(csum[...], 0, keepdims=True))
 
     def spread(msg, stats, which, mine, peer_of):
         stats[mine] = msg[...]
@@ -294,35 +347,39 @@
     lax.fori_loop(0, SIDE, diagonal_logits, 0)
     collect(rstats, 0)
 
-    def combine(stats, mine):
+    def combine(stats):
         peaks = stats[:, 0:4, :]
         totals = stats[:, 4:8, :]
         peak = jnp.max(peaks, 0)
         total = jnp.sum(totals * jnp.exp(peaks - peak[None]), 0)
-        factor = 0.5 * jnp.exp(mine[0:4, :] - peak) / total
-        return peak + jnp.log(total), factor
-
-    def line(v):
-        return jnp.concatenate([v[k:k + 1, :] for k in range(4)], 1)
-
-    row_lse, row_factor = combine(rstats, rmsg)
-    frow[...] = jnp.transpose(jnp.broadcast_to(line(row_factor), (128, TILE)), (1, 0))
+        return peak, total
+
+    row_peak, row_total = combine(rstats)
+    factors = [line(0.5 * jnp.exp(tile_peaks[d] - row_peak) / row_total) for d in range(4)]
+    frow[...] = jnp.transpose(jnp.concatenate(factors + [jnp.zeros((124, TILE), jnp.float32)], 0), (1, 0))
+    row_lse = row_peak + jnp.log(row_total)
     collect(cstats, 1)
-    col_lse, col_factor = combine(cstats, cmsg)
-    csum[0:1, :] = line(col_factor)
+    col_peak, col_total = combine(cstats)
+    cfac[0:1, :] = line(0.5 * jnp.exp(cmsg[0:4, :] - col_peak) / col_total)
+    col_lse = col_peak + jnp.log(col_total)
 
     def weigh(k, carry):
-        factor = frow[rows_of(k), :][:, 0:1]
-        w = factor * prow[rows_of(k), :] + csum[0:1, :] * pcol[rows_of(k), :]
-        weights[rows_of(k), :] = w.astype(jnp.bfloat16)
+        rows = rows_of(k)
+        for d in range(4):
+            cols = tile_cols(d)
+            w = frow[rows, d:d + 1] * prow[rows, cols] + cfac[0:1, cols] * pcol[rows, cols]
+            weights[rows, cols] = w.astype(jnp.bfloat16)
         here, slot = diagonal_slot(k)
 
         @pl.when(here)
         def _():
             cols = pair_cols(slot)
-            v = frow[rows_of(k), :] * prow[rows_of(k), cols] + csum[0:1, cols] * pcol[rows_of(k), cols]
+            lane = lax.broadcasted_iota(jnp.int32, (ROWS, 128), 1)
+            at = lax.rem(lax.div(slot, 4) - x + 4, 4)
+            factor = jnp.sum(jnp.where(lane == at, frow[rows, :], 0.0), 1, keepdims=True)
+            v = factor * prow[rows, cols] + cfac[0:1, cols] * pcol[rows, cols]
             v = v - jnp.where(pair_mask(slot), 1.0, 0.0)
-            weights[rows_of(k), cols] = v.astype(jnp.bfloat16)
+            weights[rows, cols] = v.astype(jnp.bfloat16)
 
         return carry
 
@@ -451,7 +508,7 @@
         igrad_ref[:, cols] = total
 
     text_terms(0)
-    text_swap.wait()
+    wait_on(tother, xsem.at[1])
     weight_swap.wait()
     image_terms(0)
     text_terms(1)
@@ -490,6 +547,7 @@
     wait_on(cstats.at[pl.ds(0, SIDE - 1)], small_send.at[1])
     wait_on(lstats.at[pl.ds(0, SIDE - 1)], small_send.at[2])
     wait_on(pstats.at[pl.ds(0, SIDE - 1)], small_send.at[3])
+    wait_on(tbig, xsem.at[0])
     wait_on(zin, zosend.at[0])
     wait_on(sout.at[:, pl.ds(0, 3)], ssend.at[0])
     wait_on(pout.at[:, pl.ds(0, 3)], psend.at[0])
@@ -524,6 +582,8 @@
             pltpu.VMEM((TILE, TILE), bf16),
             pltpu.VMEM((TILE, 128), f32),
             pltpu.VMEM((8, TILE), f32),
+            pltpu.VMEM((8, WIDE), f32),
+            pltpu.VMEM((8, TILE), f32),
             pltpu.VMEM((8, TILE), f32),
             pltpu.VMEM((8, 128), f32),
             pltpu.VMEM((TILE, 128), f32),
@@ -546,7 +606,7 @@
             pltpu.VMEM((2, 3, ROWS, HALF), bf16),
             pltpu.VMEM((ROWS, E), f32),
             dma((2,)), dma((1,)), dma((16,)), dma((1,)), dma((8,)),
-            dma((1,)), dma((4,)), dma((4,)), dma((4,)), dma((1,)), dma((4,)), dma((4,)),
+            dma((1,)), dma((8,)), dma((8,)), dma((8,)), dma((8,)), dma((4,)),
             dma((4,)), dma((4,)), dma((1,)), dma((5,)), dma((5,)),
             dma((1,)), dma((6,)), dma((1,)), dma((6,)),
         ],

time: 77.9 us -> 87.2 us (1.12)
  Pallas kernels: 72.2 us -> 81.5 us
    pallas_call x1, Pallas kernels: 72.2 us -> 81.5 us  [per_device(): pl.pallas_call(kernel, out_shape=(jax.ShapeDtypeStruct((1, 1), f32), jax....]
where the time goes in v3:
time: 87.2 us; the launch traced here: 87.1 us
  Pallas kernels  81.5 us (93%)
  between operations  3.1 us (4%)
  local copies, waits for them, and re-layouts  2.45 us (3%)
    pallas_call x1, Pallas kernels, per_device(): pl.pallas_call(kernel, out_shape=(jax.ShapeDtypeStruct((1, 1), f32), jax....  81.5 us
    unnamed x4, local copies, waits for them, and re-layouts  2.45 us

profile of v3, /device:TPU:1, one launch (start us, length us, event | category | flops | bytes accessed | tf_op | source)
XLA Modules:
  0.0 87.1 jit_solution(14514282693226618796)
XLA Ops:
  1.3 81.5 %shard_map.58 = (f32[1,1]{1,0:T(1,128)}, f32[56,1280]{1,0:T(8,128)}, f32[56,1280]{1,0:T(8,128)}) custom-call(bf16[56,1280]{1,0:T(8,128)(2,1)} %images_ref.1, bf16[56,1280]{1,0:T(8,128)(2,1)} %texts_ref.1, f32[1]{0:T(128)S(6)} %copy.9.scale_ref), custom_call_target="tpu_custom_call" | custom-call | tf_op jit(solution)/shard_map/pallas_call | solution.py:562
  83.5 0.0 copy-start
  83.5 1.7 %copy.11 = f32[56,1280]{1,0:T(8,128)} copy(f32[56,1280]{1,0:T(8,128)} %get-tuple-element.13) | data formatting | bytes 573440
  85.2 0.0 copy-done
  85.2 0.7 copy.12
Async XLA Ops:
  83.5 1.7 %copy-start = (f32[56,1280]{1,0:T(8,128)S(1)}, f32[56,1280]{1,0:T(8,128)}, u32[]{:S(2)}) copy-start(f32[56,1280]{1,0:T(8,128)} %get-tuple-element.14) | copy-start | bytes 860164

commit v4 on v2

--- a/solution.py
+++ b/solution.py
@@ -35,10 +35,10 @@
 def kernel(
     images_ref, texts_ref, scale_ref,
     loss_ref, igrad_ref, tgrad_ref,
-    ibuf, tbuf, ibig, tbig, tother, logits, prow, pcol, weights, wother, wturned,
+    stage, ibig, tbig, tother, logits, prow, pcol, weights, wother, wturned,
     rsub, csum, cmax, dsum, frow, rmsg, cmsg, rstats, cstats, lmsg, lstats, pmsg, pstats,
     ipart, tpart, zout, zagg, zin, sout, sin, pout, pin, pkeep,
-    own_sem, zsend, zrecv, isend, icross, tsend, ta0, ta1, tb0, tb1, tc, xsem,
+    own_sem, zsend, zrecv, isend, icross, tsend, tfirst, tplus, tminus, tfar, xsem,
     small_send, small_recv, zosend, zfirst, zlast, ssend, srecv, psend, precv,
 ):
     img = lax.axis_index("img")
@@ -87,50 +87,92 @@
         return carry
 
     lax.fori_loop(1, SIDE, greet, 0)
-    own_image = pltpu.make_async_copy(images_ref, ibuf.at[islot], own_sem.at[0])
-    own_text = pltpu.make_async_copy(texts_ref, tbuf.at[tslot], own_sem.at[1])
+    own_image = pltpu.make_async_copy(images_ref, stage.at[0], own_sem.at[0])
+    own_text = pltpu.make_async_copy(texts_ref, stage.at[1], own_sem.at[1])
     own_image.start()
     own_text.start()
-    ibig[...] = jnp.zeros_like(ibig)
-    tbig[...] = jnp.zeros_like(tbig)
+
+    def block_rows(slot):
+        return pl.ds(pl.multiple_of(slot * PITCH, PITCH), PITCH)
+
+    ibig[block_rows(islot), :] = jnp.zeros((PITCH, E), jnp.bfloat16)
+    tbig[block_rows(tslot), :] = jnp.zeros((PITCH, E), jnp.bfloat16)
     own_image.wait()
     own_text.wait()
+    ibig[pl.ds(pl.multiple_of(islot * PITCH, PITCH), ROWS), :] = stage[0]
+    tbig[pl.ds(pl.multiple_of(tslot * PITCH, PITCH), ROWS), :] = stage[1]
     pl.semaphore_wait(barrier, 2 * (SIDE - 1))
 
-    def half_of(buf, slot, half):
-        return buf.at[slot, :, pl.ds(half * HALF, HALF)]
-
-    def z_copy(owner, way, half):
-        ref = half_of(ibuf, c * 8 + owner, half)
-        return copy(ref, ref, zsend.at[0], zrecv.at[half * 8 + owner], device(x, y, z_at(1 if way == 0 else -1), c))
+    def half_of(big, slot, half):
+        return big.at[block_rows(slot), pl.ds(half * HALF, HALF)]
+
+    def z_copy(owner, way, half, far=False):
+        ref = half_of(ibig, c * 8 + owner, half)
+        d = 2 if far else 1
+        return copy(ref, ref, zsend.at[0], zrecv.at[half * 8 + owner], device(x, y, z_at(d if way == 0 else -d), c))
 
     def z_wait(owner, half):
-        wait_on(half_of(ibuf, c * 8 + owner, half), zrecv.at[half * 8 + owner])
-
-    def cross_copy(owner):
-        ref = ibuf.at[c * 8 + owner]
-        return copy(ref, ref, isend.at[0], icross.at[owner], twin)
-
-    def t_copy(slot, half, sem, where):
-        ref = half_of(tbuf, slot, half)
-        return copy(ref, ref, tsend.at[0], sem, where)
-
-    def place(buf, big, slot):
-        big[pl.ds(pl.multiple_of(slot * PITCH, PITCH), ROWS), :] = buf[slot]
-
+        wait_on(half_of(ibig, c * 8 + owner, half), zrecv.at[half * 8 + owner])
+
+    def cross_copy(owner, half):
+        ref = half_of(ibig, c * 8 + owner, half)
+        copy(ref, ref, isend.at[0], icross.at[half * 8 + owner], twin).start()
+
+    def t_slot(half, u, v):
+        return u * 4 + v if half == 0 else v * 4 + u
+
+    def t_here(half):
+        return (x, y) if half == 0 else (y, x)
+
+    def t_device(half, u, v):
+        return device(u, v, z, c) if half == 0 else device(v, u, z, c)
+
+    def t_send(half, u, v, sem, to_u, to_v):
+        ref = half_of(tbig, t_slot(half, u, v), half)
+        copy(ref, ref, tsend.at[0], sem.at[half * 4 + u], t_device(half, to_u, to_v)).start()
+
+    def t_wait(half, u, v, sem):
+        wait_on(half_of(tbig, t_slot(half, u, v), half), sem.at[half * 4 + u])
+
+    def t_first(half):
+        u, v = t_here(half)
+        for d in NEAR:
+            t_send(half, u, v, tfirst, lax.rem(u + d, 4), v)
+
+    def t_second(half, d):
+        u, v = t_here(half)
+        there = lax.rem(u + d, 4)
+        if d:
+            t_wait(half, there, v, tfirst)
+        t_send(half, there, v, tplus, u, lax.rem(v + 1, 4))
+        t_send(half, there, v, tminus, u, lax.rem(v + 3, 4))
+
+    def t_pass(half, d):
+        u, v = t_here(half)
+        there = lax.rem(u + d, 4)
+        before = lax.rem(v + 3, 4)
+        after = lax.rem(v + 1, 4)
+        t_wait(half, there, before, tplus)
+        if d < 2:
+            t_send(half, there, before, tfar, u, after)
+        t_wait(half, there, after, tminus)
+        if d >= 2:
+            t_send(half, there, after, tfar, u, before)
+
+    def t_last(half, d):
+        u, v = t_here(half)
+        t_wait(half, lax.rem(u + d, 4), lax.rem(v + 2, 4), tfar)
+
+    t_first(0)
+    t_first(1)
     z_copy(z, 0, 0).start()
     z_copy(z, 1, 0).start()
-    for d in NEAR:
-        t_copy(tslot, 0, ta0.at[x], device(x_at(d), y, z, c)).start()
-        t_copy(tslot, 1, ta1.at[y], device(x, y_at(d), z, c)).start()
+    t_second(0, 0)
+    t_second(1, 0)
     z_copy(z, 0, 1).start()
     z_copy(z, 1, 1).start()
-    for d in NEAR:
-        t_copy(tslot, 1, tb0.at[x], device(x_at(d), y, z, c)).start()
-        t_copy(tslot, 0, tb1.at[0], device(x, y_at(d), z, c)).start()
-    cross_copy(z).start()
-    place(ibuf, ibig, islot)
-    place(tbuf, tbig, tslot)
+    cross_copy(z, 0)
+    cross_copy(z, 1)
     weights[...] = jnp.zeros_like(weights)
     rsub[...] = jnp.zeros_like(rsub)
 
@@ -140,77 +182,65 @@
         z_wait(left, half)
         if step < 2:
             z_copy(left, 0, half).start()
-        else:
+        if step == 1:
             @pl.when(c == 0)
             def _():
-                z_copy(left, 0, half).start()
+                z_copy(left, 0, half, True).start()
+        cross_copy(left, half)
         z_wait(right, half)
         if step < 2:
             z_copy(right, 1, half).start()
-        else:
+        if step == 1:
             @pl.when(c == 1)
             def _():
-                z_copy(right, 1, half).start()
-        if half == 1:
-            cross_copy(left).start()
-            cross_copy(right).start()
-            place(ibuf, ibig, c * 8 + left)
-            place(ibuf, ibig, c * 8 + right)
-
-    def t_step(d):
-        slot0 = x_at(d) * 4 + y
-        slot1 = x * 4 + y_at(d)
-        wait_on(half_of(tbuf, slot0, 0), ta0.at[x_at(d)])
-        for e in NEAR:
-            t_copy(slot0, 0, tc.at[x_at(d)], device(x, y_at(e), z, c)).start()
-        wait_on(half_of(tbuf, slot1, 1), ta1.at[y_at(d)])
-        for e in NEAR:
-            t_copy(slot1, 1, tc.at[x], device(x_at(e), y, z, c)).start()
+                z_copy(right, 1, half, True).start()
+        cross_copy(right, half)
+
+    def t_both(what, d):
+        what(0, d)
+        what(1, d)
 
     z_step(0, 0)
-    t_step(1)
+    t_both(t_second, 1)
     z_step(0, 1)
-    t_step(3)
+    t_both(t_second, 3)
+    t_both(t_pass, 0)
     z_step(1, 0)
-    t_step(2)
+    t_both(t_second, 2)
+    t_both(t_pass, 1)
     z_step(1, 1)
+    t_both(t_pass, 3)
     z_step(2, 0)
+    t_both(t_pass, 2)
     z_step(2, 1)
-    far = z_at(4)
-    z_wait(far, 0)
-    z_wait(far, 1)
-    cross_copy(far).start()
-    place(ibuf, ibig, c * 8 + far)
-    wait_on(tbuf.at[pl.ds(0, 3), :, pl.ds(0, HALF)], tb1.at[0])
-    for d in NEAR:
-        place(tbuf, tbig, x * 4 + y_at(d))
+    for half in range(2):
+        z_wait(z_at(4), half)
+        cross_copy(z_at(4), half)
+    t_both(t_last, 0)
+    t_both(t_last, 1)
+    t_both(t_last, 3)
+    t_both(t_last, 2)
+    text_swap = copy(tbig, tother, xsem.at[0], xsem.at[1], twin)
 
     def other_image(k, carry):
-        wait_on(ibuf.at[oc * 8 + k], icross.at[k])
-        place(ibuf, ibig, oc * 8 + k)
+        wait_on(half_of(ibig, oc * 8 + k, 0), icross.at[k])
+        wait_on(half_of(ibig, oc * 8 + k, 1), icross.at[8 + k])
         return carry
 
     lax.fori_loop(0, 8, other_image, 0)
 
     scale = scale_ref[0]
 
-    def score(tile):
+    def score(tile, carry):
         cols = pl.ds(pl.multiple_of(tile * WIDE, WIDE), WIDE)
         part = lax.dot_general(
             ibig[...], tbig[cols, :], (((1,), (1,)), ((), ())), preferred_element_type=jnp.float32
         )
         pad = lax.bitwise_and(lax.broadcasted_iota(jnp.int32, (1, WIDE), 1), PITCH - 1) >= ROWS
         logits[:, cols] = jnp.where(pad, FLOOR, part * scale)
-
-    score(x)
-    for d in NEAR:
-        tile = x_at(d)
-        wait_on(half_of(tbuf, tile * 4 + y, 1), tb0.at[tile])
-        wait_on(tbuf.at[pl.ds(0, 3)], tc.at[tile])
-        for e in range(4):
-            place(tbuf, tbig, tile * 4 + e)
-        score(tile)
-    text_swap = copy(tbig, tother, xsem.at[0], xsem.at[1], twin)
+        return carry
+
+    lax.fori_loop(0, 4, score, 0)
     text_swap.start()
 
     def rows_of(k):
@@ -226,20 +256,27 @@
     col_top = jnp.max(cmax[...], 0, keepdims=True)
     csum[...] = jnp.zeros_like(csum)
 
-    def exponentials(k, carry):
-        part = logits[rows_of(k), :]
-        top = jnp.max(part, 1, keepdims=True)
-        by_row = jnp.exp(part - top)
-        by_col = jnp.exp(part - col_top)
-        prow[rows_of(k), :] = by_row
-        pcol[rows_of(k), :] = by_col
-        total = jnp.sum(by_row, 1, keepdims=True)
-        first = lax.broadcasted_iota(jnp.int32, (ROWS, 128), 1) == 0
-        rsub[rows_of(k), :] = jnp.where(first, top, total)
-        csum[...] += jnp.sum(by_col.reshape(7, 8, TILE), 0)
+    first = lax.broadcasted_iota(jnp.int32, (ROWS, 128), 1) == 0
+
+    def exponentials(g, carry):
+        blocks = [rows_of(4 * g + q) for q in range(4)]
+        tops = [jnp.max(logits[rows, :], 1, keepdims=True) for rows in blocks]
+        added = jnp.zeros((8, TILE), jnp.float32)
+        totals = []
+        for rows, top in zip(blocks, tops):
+            part = logits[rows, :]
+            by_row = jnp.exp(part - top)
+            by_col = jnp.exp(part - col_top)
+            prow[rows, :] = by_row
+            pcol[rows, :] = by_col
+            added = added + jnp.sum(by_col.reshape(7, 8, TILE), 0)
+            totals.append(jnp.sum(by_row, 1, keepdims=True))
+        for rows, top, total in zip(blocks, tops, totals):
+            rsub[rows, :] = jnp.where(first, top, total)
+        csum[...] += added
         return carry
 
-    lax.fori_loop(0, SIDE, exponentials, 0)
+    lax.fori_loop(0, SIDE // 4, exponentials, 0)
 
     row_stats = jnp.transpose(rsub[...], (1, 0))
     col_total_here = jnp.sum(csum[...], 0, keepdims=True)
@@ -483,9 +520,9 @@
     collect(pstats, 3)
     loss_ref[...] = (jnp.sum(pstats[...], 0) / (2.0 * PAIRS))[0:1, 0:1]
 
-    wait_on(ibuf.at[pl.ds(0, 7)], zsend.at[0])
-    wait_on(ibuf.at[pl.ds(0, 8)], isend.at[0])
-    wait_on(tbuf.at[pl.ds(0, 15)], tsend.at[0])
+    wait_on(ibig.at[pl.ds(0, 7 * PITCH), :], zsend.at[0])
+    wait_on(ibig.at[pl.ds(0, 8 * PITCH), :], isend.at[0])
+    wait_on(tbig.at[pl.ds(0, 15 * PITCH), :], tsend.at[0])
     wait_on(rstats.at[pl.ds(0, SIDE - 1)], small_send.at[0])
     wait_on(cstats.at[pl.ds(0, SIDE - 1)], small_send.at[1])
     wait_on(lstats.at[pl.ds(0, SIDE - 1)], small_send.at[2])
@@ -511,8 +548,7 @@
         in_specs=[hbm, hbm, smem],
         out_specs=(vmem, vmem, vmem),
         scratch_shapes=[
-            pltpu.VMEM((SIDE, ROWS, E), bf16),
-            pltpu.VMEM((SIDE, ROWS, E), bf16),
+            pltpu.VMEM((2, ROWS, E), bf16),
             pltpu.VMEM((TILE, E), bf16),
             pltpu.VMEM((TILE, E), bf16),
             pltpu.VMEM((TILE, E), bf16),
@@ -545,8 +581,8 @@
             pltpu.VMEM((2, 4, ROWS, HALF), bf16),
             pltpu.VMEM((2, 3, ROWS, HALF), bf16),
             pltpu.VMEM((ROWS, E), f32),
-            dma((2,)), dma((1,)), dma((16,)), dma((1,)), dma((8,)),
-            dma((1,)), dma((4,)), dma((4,)), dma((4,)), dma((1,)), dma((4,)), dma((4,)),
+            dma((2,)), dma((1,)), dma((16,)), dma((1,)), dma((16,)),
+            dma((1,)), dma((8,)), dma((8,)), dma((8,)), dma((8,)), dma((4,)),
             dma((4,)), dma((4,)), dma((1,)), dma((5,)), dma((5,)),
             dma((1,)), dma((6,)), dma((1,)), dma((6,)),
         ],

time: 77.9 us -> 74.2 us (0.953)
  Pallas kernels: 72.2 us -> 68.5 us
    pallas_call x1, Pallas kernels: 72.2 us -> 68.5 us  [per_device(): pl.pallas_call(kernel, out_shape=(jax.ShapeDtypeStruct((1, 1), f32), jax....]
where the time goes in v4:
time: 74.2 us; the launch traced here: 74.1 us
  Pallas kernels  68.5 us (92%)
  between operations  3.1 us (4%)
  local copies, waits for them, and re-layouts  2.45 us (3%)
    pallas_call x1, Pallas kernels, per_device(): pl.pallas_call(kernel, out_shape=(jax.ShapeDtypeStruct((1, 1), f32), jax....  68.5 us
    unnamed x4, local copies, waits for them, and re-layouts  2.45 us

profile of v4, /device:TPU:1, one launch (start us, length us, event | category | flops | bytes accessed | tf_op | source)
XLA Modules:
  0.0 74.1 jit_solution(1760560111605281287)
XLA Ops:
  1.3 68.5 %shard_map.58 = (f32[1,1]{1,0:T(1,128)}, f32[56,1280]{1,0:T(8,128)}, f32[56,1280]{1,0:T(8,128)}) custom-call(bf16[56,1280]{1,0:T(8,128)(2,1)} %images_ref.1, bf16[56,1280]{1,0:T(8,128)(2,1)} %texts_ref.1, f32[1]{0:T(128)S(6)} %copy.9.scale_ref), custom_call_target="tpu_custom_call" | custom-call | tf_op jit(solution)/shard_map/pallas_call | solution.py:541
  70.5 0.0 copy-start
  70.5 1.7 %copy.11 = f32[56,1280]{1,0:T(8,128)} copy(f32[56,1280]{1,0:T(8,128)} %get-tuple-element.13) | data formatting | bytes 573440
  72.2 0.0 copy-done
  72.2 0.7 copy.12
Async XLA Ops:
  70.5 1.7 %copy-start = (f32[56,1280]{1,0:T(8,128)S(1)}, f32[56,1280]{1,0:T(8,128)}, u32[]{:S(2)}) copy-start(f32[56,1280]{1,0:T(8,128)} %get-tuple-element.14) | copy-start | bytes 860164

commit v5 on v4

--- a/solution.py
+++ b/solution.py
@@ -144,6 +144,8 @@
         there = lax.rem(u + d, 4)
         if d:
             t_wait(half, there, v, tfirst)
+        if d == 2:
+            t_send(half, there, v, tfar, u, lax.rem(v + 2, 4))
         t_send(half, there, v, tplus, u, lax.rem(v + 1, 4))
         t_send(half, there, v, tminus, u, lax.rem(v + 3, 4))
 
@@ -156,7 +158,7 @@
         if d < 2:
             t_send(half, there, before, tfar, u, after)
         t_wait(half, there, after, tminus)
-        if d >= 2:
+        if d == 3:
             t_send(half, there, after, tfar, u, before)
 
     def t_last(half, d):
@@ -180,20 +182,20 @@
         left = z_at(-1 - step)
         right = z_at(1 + step)
         z_wait(left, half)
-        if step < 2:
-            z_copy(left, 0, half).start()
         if step == 1:
             @pl.when(c == 0)
             def _():
                 z_copy(left, 0, half, True).start()
+        if step < 2:
+            z_copy(left, 0, half).start()
         cross_copy(left, half)
         z_wait(right, half)
-        if step < 2:
-            z_copy(right, 1, half).start()
         if step == 1:
             @pl.when(c == 1)
             def _():
                 z_copy(right, 1, half, True).start()
+        if step < 2:
+            z_copy(right, 1, half).start()
         cross_copy(right, half)
 
     def t_both(what, d):
@@ -202,17 +204,17 @@
 
     z_step(0, 0)
     t_both(t_second, 1)
+    t_both(t_second, 3)
     z_step(0, 1)
-    t_both(t_second, 3)
+    t_both(t_second, 2)
+    z_step(1, 0)
     t_both(t_pass, 0)
-    z_step(1, 0)
-    t_both(t_second, 2)
+    z_step(1, 1)
     t_both(t_pass, 1)
-    z_step(1, 1)
     t_both(t_pass, 3)
     z_step(2, 0)
+    z_step(2, 1)
     t_both(t_pass, 2)
-    z_step(2, 1)
     for half in range(2):
         z_wait(z_at(4), half)
         cross_copy(z_at(4), half)
@@ -462,6 +464,10 @@
         image_send(n, zout.at[z_at(4), :, pl.ds(low + 128, 128)], 2, low + 128, 128, zfirst, -2).start()
         image_send(n, zout.at[z_at(3), :, cols], 0, low, WIDE, zfirst, 1).start()
         image_send(n, zout.at[z_at(-3), :, cols], 1, low, WIDE, zfirst, -1).start()
+
+    def image_near(n):
+        low = n * WIDE
+        cols = pl.ds(low, WIDE)
         image_send(n, zout.at[z_at(1), :, cols], 3, low, WIDE, zlast, 1).start()
         image_send(n, zout.at[z_at(-1), :, cols], 4, low, WIDE, zlast, -1).start()
 
@@ -488,29 +494,34 @@
         igrad_ref[:, cols] = total
 
     text_terms(0)
+    text_terms(1)
     text_swap.wait()
     weight_swap.wait()
     image_terms(0)
-    text_terms(1)
     image_terms(1)
-    image_second(0)
     text_terms(2)
+    text_terms(3)
     image_terms(2)
-    image_second(1)
-    text_second(0)
-    text_terms(3)
     image_terms(3)
-    image_second(2)
-    text_second(1)
     text_terms(4)
     image_terms(4)
+    image_second(0)
+    image_near(0)
+    text_second(0)
+    image_second(1)
+    image_near(1)
+    text_second(1)
+    image_second(2)
+    image_near(2)
+    text_second(2)
     image_second(3)
-    text_second(2)
+    image_near(3)
+    text_second(3)
     collect(lstats, 2)
     pmsg[...] = jnp.sum(lstats[...], 0)
     spread(pmsg, pstats, 3, tslot, col_peer)
     image_second(4)
-    text_second(3)
+    image_near(4)
     text_second(4)
     text_second(5)
     for n in range(CHUNKS):

time: 74.2 us -> 75.9 us (1.023)
  Pallas kernels: 68.5 us -> 70.2 us
    pallas_call x1, Pallas kernels: 68.5 us -> 70.2 us  [per_device(): pl.pallas_call(kernel, out_shape=(jax.ShapeDtypeStruct((1, 1), f32), jax....]
where the time goes in v5:
time: 75.9 us; the launch traced here: 75.7 us
  Pallas kernels  70.2 us (92%)
  between operations  3.1 us (4%)
  local copies, waits for them, and re-layouts  2.45 us (3%)
    pallas_call x1, Pallas kernels, per_device(): pl.pallas_call(kernel, out_shape=(jax.ShapeDtypeStruct((1, 1), f32), jax....  70.2 us
    unnamed x4, local copies, waits for them, and re-layouts  2.45 us

profile of v5, /device:TPU:1, one launch (start us, length us, event | category | flops | bytes accessed | tf_op | source)
XLA Modules:
  0.0 75.7 jit_solution(10122257166281768561)
XLA Ops:
  1.3 70.2 %shard_map.58 = (f32[1,1]{1,0:T(1,128)}, f32[56,1280]{1,0:T(8,128)}, f32[56,1280]{1,0:T(8,128)}) custom-call(bf16[56,1280]{1,0:T(8,128)(2,1)} %images_ref.1, bf16[56,1280]{1,0:T(8,128)(2,1)} %texts_ref.1, f32[1]{0:T(128)S(6)} %copy.9.scale_ref), custom_call_target="tpu_custom_call" | custom-call | tf_op jit(solution)/shard_map/pallas_call | solution.py:552
  72.1 0.0 copy-start
  72.1 1.7 %copy.11 = f32[56,1280]{1,0:T(8,128)} copy(f32[56,1280]{1,0:T(8,128)} %get-tuple-element.13) | data formatting | bytes 573440
  73.9 0.0 copy-done
  73.9 0.7 copy.12
Async XLA Ops:
  72.1 1.7 %copy-start = (f32[56,1280]{1,0:T(8,128)S(1)}, f32[56,1280]{1,0:T(8,128)}, u32[]{:S(2)}) copy-start(f32[56,1280]{1,0:T(8,128)} %get-tuple-element.14) | copy-start | bytes 860164

commit v6 on v5

--- a/solution.py
+++ b/solution.py
@@ -17,13 +17,8 @@
 CHUNKS = E // WIDE
 HALF = 640
 FLOOR = -1e30
-PIECES = (
-    (0, 0, 256, 0),
-    (1, 256, 256, 0),
-    (0, 512, 256, 256),
-    (1, 768, 256, 256),
-    (0, 1024, 128, 512),
-    (1, 1152, 128, 512),
+PIECES = tuple(
+    (axis, n * WIDE + axis * 128, 128, n * 128) for n in range(CHUNKS) for axis in range(2)
 )
 NEAR = (1, 3, 2)
 
@@ -493,41 +488,43 @@
             total = total + zin[k, :, cols].astype(jnp.float32)
         igrad_ref[:, cols] = total
 
+    def both_second(n):
+        image_second(n)
+        image_near(n)
+
+    def text_both(n):
+        text_second(2 * n)
+        text_second(2 * n + 1)
+
     text_terms(0)
-    text_terms(1)
     text_swap.wait()
     weight_swap.wait()
     image_terms(0)
+    text_terms(1)
     image_terms(1)
+    both_second(0)
     text_terms(2)
+    image_terms(2)
+    text_both(0)
+    both_second(1)
     text_terms(3)
-    image_terms(2)
     image_terms(3)
+    text_both(1)
+    both_second(2)
     text_terms(4)
     image_terms(4)
-    image_second(0)
-    image_near(0)
-    text_second(0)
-    image_second(1)
-    image_near(1)
-    text_second(1)
-    image_second(2)
-    image_near(2)
-    text_second(2)
-    image_second(3)
-    image_near(3)
-    text_second(3)
+    text_both(2)
+    both_second(3)
     collect(lstats, 2)
     pmsg[...] = jnp.sum(lstats[...], 0)
     spread(pmsg, pstats, 3, tslot, col_peer)
-    image_second(4)
-    image_near(4)
-    text_second(4)
-    text_second(5)
+    both_second(4)
+    text_both(3)
+    text_both(4)
     for n in range(CHUNKS):
         image_last(n)
-        text_last(n)
-    text_last(5)
+        text_last(2 * n)
+        text_last(2 * n + 1)
     collect(pstats, 3)
     loss_ref[...] = (jnp.sum(pstats[...], 0) / (2.0 * PAIRS))[0:1, 0:1]
 
@@ -595,7 +592,7 @@
             dma((2,)), dma((1,)), dma((16,)), dma((1,)), dma((16,)),
             dma((1,)), dma((8,)), dma((8,)), dma((8,)), dma((8,)), dma((4,)),
             dma((4,)), dma((4,)), dma((1,)), dma((5,)), dma((5,)),
-            dma((1,)), dma((6,)), dma((1,)), dma((6,)),
+            dma((1,)), dma((10,)), dma((1,)), dma((10,)),
         ],
         compiler_params=pltpu.CompilerParams(
             collective_id=0, has_side_effects=True, vmem_limit_bytes=60 * 1024 * 1024

time: 75.9 us -> 72.4 us (0.954)
  Pallas kernels: 70.2 us -> 66.3 us
    pallas_call x1, Pallas kernels: 70.2 us -> 66.3 us  [per_device(): pl.pallas_call(kernel, out_shape=(jax.ShapeDtypeStruct((1, 1), f32), jax....]
where the time goes in v6:
time: 72.4 us; the launch traced here: 71.9 us
  Pallas kernels  66.3 us (92%)
  between operations  3.1 us (4%)
  local copies, waits for them, and re-layouts  2.45 us (3%)
    pallas_call x1, Pallas kernels, per_device(): pl.pallas_call(kernel, out_shape=(jax.ShapeDtypeStruct((1, 1), f32), jax....  66.3 us
    unnamed x4, local copies, waits for them, and re-layouts  2.45 us

profile of v6, /device:TPU:1, one launch (start us, length us, event | category | flops | bytes accessed | tf_op | source)
XLA Modules:
  0.0 71.9 jit_solution(9786113437526904509)
XLA Ops:
  1.3 66.3 %shard_map.58 = (f32[1,1]{1,0:T(1,128)}, f32[56,1280]{1,0:T(8,128)}, f32[56,1280]{1,0:T(8,128)}) custom-call(bf16[56,1280]{1,0:T(8,128)(2,1)} %images_ref.1, bf16[56,1280]{1,0:T(8,128)(2,1)} %texts_ref.1, f32[1]{0:T(128)S(6)} %copy.9.scale_ref), custom_call_target="tpu_custom_call" | custom-call | tf_op jit(solution)/shard_map/pallas_call | solution.py:549
  68.3 0.0 copy-start
  68.3 1.7 %copy.11 = f32[56,1280]{1,0:T(8,128)} copy(f32[56,1280]{1,0:T(8,128)} %get-tuple-element.13) | data formatting | bytes 573440
  70.0 0.0 copy-done
  70.0 0.7 copy.12
Async XLA Ops:
  68.3 1.7 %copy-start = (f32[56,1280]{1,0:T(8,128)S(1)}, f32[56,1280]{1,0:T(8,128)}, u32[]{:S(2)}) copy-start(f32[56,1280]{1,0:T(8,128)} %get-tuple-element.14) | copy-start | bytes 860164

commit v7 on v6

--- a/solution.py
+++ b/solution.py
@@ -217,86 +217,94 @@
     t_both(t_last, 1)
     t_both(t_last, 3)
     t_both(t_last, 2)
-    text_swap = copy(tbig, tother, xsem.at[0], xsem.at[1], twin)
+    scale = scale_ref[0]
+
+    def score(tile, lane_rows):
+        cols = pl.ds(pl.multiple_of(tile * WIDE, WIDE), WIDE)
+        rows = pl.ds(pl.multiple_of(lane_rows, CORE), CORE)
+        part = lax.dot_general(
+            ibig[rows, :], tbig[cols, :], (((1,), (1,)), ((), ())), preferred_element_type=jnp.float32
+        )
+        pad = lax.bitwise_and(lax.broadcasted_iota(jnp.int32, (1, WIDE), 1), PITCH - 1) >= ROWS
+        logits[rows, cols] = jnp.where(pad, FLOOR, part * scale)
+        return lane_rows
 
     def other_image(k, carry):
         wait_on(half_of(ibig, oc * 8 + k, 0), icross.at[k])
         wait_on(half_of(ibig, oc * 8 + k, 1), icross.at[8 + k])
         return carry
 
+    lax.fori_loop(0, 4, score, c * CORE)
     lax.fori_loop(0, 8, other_image, 0)
-
-    scale = scale_ref[0]
-
-    def score(tile, carry):
-        cols = pl.ds(pl.multiple_of(tile * WIDE, WIDE), WIDE)
-        part = lax.dot_general(
-            ibig[...], tbig[cols, :], (((1,), (1,)), ((), ())), preferred_element_type=jnp.float32
-        )
-        pad = lax.bitwise_and(lax.broadcasted_iota(jnp.int32, (1, WIDE), 1), PITCH - 1) >= ROWS
-        logits[:, cols] = jnp.where(pad, FLOOR, part * scale)
-        return carry
-
-    lax.fori_loop(0, 4, score, 0)
+    lax.fori_loop(0, 4, score, oc * CORE)
+    text_swap = copy(tbig, tother, xsem.at[0], xsem.at[1], twin)
     text_swap.start()
 
     def rows_of(k):
         return pl.ds(pl.multiple_of(k * PITCH, PITCH), ROWS)
 
     cmax[...] = jnp.full_like(cmax, FLOOR)
-
-    def col_max(k, carry):
-        cmax[...] = jnp.maximum(cmax[...], jnp.max(logits[rows_of(k), :].reshape(7, 8, TILE), 0))
+    first = lax.broadcasted_iota(jnp.int32, (ROWS, 128), 1) == 0
+
+    def four(g):
+        return [rows_of(4 * g + q) for q in range(4)]
+
+    def row_part(g, carry):
+        tops = []
+        peak = cmax[...]
+        for rows in four(g):
+            part = logits[rows, :]
+            tops.append(jnp.max(part, 1, keepdims=True))
+            peak = jnp.maximum(peak, jnp.max(part.reshape(7, 8, TILE), 0))
+        totals = []
+        for rows, top in zip(four(g), tops):
+            by_row = jnp.exp(logits[rows, :] - top)
+            prow[rows, :] = by_row
+            totals.append(jnp.sum(by_row, 1, keepdims=True))
+        for rows, top, total in zip(four(g), tops, totals):
+            rsub[rows, :] = jnp.where(first, top, total)
+        cmax[...] = peak
         return carry
 
-    lax.fori_loop(0, SIDE, col_max, 0)
-    col_top = jnp.max(cmax[...], 0, keepdims=True)
-    csum[...] = jnp.zeros_like(csum)
-
-    first = lax.broadcasted_iota(jnp.int32, (ROWS, 128), 1) == 0
-
-    def exponentials(g, carry):
-        blocks = [rows_of(4 * g + q) for q in range(4)]
-        tops = [jnp.max(logits[rows, :], 1, keepdims=True) for rows in blocks]
-        added = jnp.zeros((8, TILE), jnp.float32)
-        totals = []
-        for rows, top in zip(blocks, tops):
-            part = logits[rows, :]
-            by_row = jnp.exp(part - top)
-            by_col = jnp.exp(part - col_top)
-            prow[rows, :] = by_row
-            pcol[rows, :] = by_col
-            added = added + jnp.sum(by_col.reshape(7, 8, TILE), 0)
-            totals.append(jnp.sum(by_row, 1, keepdims=True))
-        for rows, top, total in zip(blocks, tops, totals):
-            rsub[rows, :] = jnp.where(first, top, total)
-        csum[...] += added
-        return carry
-
-    lax.fori_loop(0, SIDE // 4, exponentials, 0)
+    lax.fori_loop(0, SIDE // 4, row_part, 0)
+
+    def spread(msg, stats, which, mine, peer_of):
+        stats[mine] = msg[...]
+
+        def send(k, carry):
+            copy(msg, stats.at[mine], small_send.at[which], small_recv.at[which], peer_of(lax.rem(mine + k, SIDE))).start()
+            return carry
+
+        lax.fori_loop(1, SIDE, send, 0)
+
+    def collect(stats, which):
+        wait_on(stats.at[pl.ds(0, SIDE - 1)], small_recv.at[which])
 
     row_stats = jnp.transpose(rsub[...], (1, 0))
-    col_total_here = jnp.sum(csum[...], 0, keepdims=True)
     for k in range(4):
         part = slice(k * WIDE, (k + 1) * WIDE)
         rmsg[k:k + 1, :] = row_stats[0:1, part]
         rmsg[4 + k:5 + k, :] = row_stats[1:2, part]
+    spread(rmsg, rstats, 0, islot, row_peer)
+
+    col_top = jnp.max(cmax[...], 0, keepdims=True)
+    csum[...] = jnp.zeros_like(csum)
+
+    def col_part(g, carry):
+        added = csum[...]
+        for rows in four(g):
+            by_col = jnp.exp(logits[rows, :] - col_top)
+            pcol[rows, :] = by_col
+            added = added + jnp.sum(by_col.reshape(7, 8, TILE), 0)
+        csum[...] = added
+        return carry
+
+    lax.fori_loop(0, SIDE // 4, col_part, 0)
+    col_total_here = jnp.sum(csum[...], 0, keepdims=True)
+    for k in range(4):
+        part = slice(k * WIDE, (k + 1) * WIDE)
         cmsg[k:k + 1, :] = col_top[:, part]
         cmsg[4 + k:5 + k, :] = col_total_here[:, part]
-
-    def spread(msg, stats, which, mine, peer_of):
-        stats[mine] = msg[...]
-
-        def send(k, carry):
-            copy(msg, stats.at[mine], small_send.at[which], small_recv.at[which], peer_of(lax.rem(mine + k, SIDE))).start()
-            return carry
-
-        lax.fori_loop(1, SIDE, send, 0)
-
-    def collect(stats, which):
-        wait_on(stats.at[pl.ds(0, SIDE - 1)], small_recv.at[which])
-
-    spread(rmsg, rstats, 0, islot, row_peer)
     spread(cmsg, cstats, 1, tslot, col_peer)
 
     def diagonal_slot(k):

time: 72.4 us -> 72.9 us (level)
  no operation moved by 1% of the time
where the time goes in v7:
time: 72.9 us; the launch traced here: 71.9 us
  Pallas kernels  66.4 us (91%)
  between operations  3.1 us (4%)
  local copies, waits for them, and re-layouts  2.45 us (3%)
    pallas_call x1, Pallas kernels, per_device(): pl.pallas_call(kernel, out_shape=(jax.ShapeDtypeStruct((1, 1), f32), jax....  66.4 us
    unnamed x4, local copies, waits for them, and re-layouts  2.45 us

profile of v7, /device:TPU:1, one launch (start us, length us, event | category | flops | bytes accessed | tf_op | source)
XLA Modules:
  0.0 71.9 jit_solution(4928388880850544650)
XLA Ops:
  1.3 66.4 %shard_map.58 = (f32[1,1]{1,0:T(1,128)}, f32[56,1280]{1,0:T(8,128)}, f32[56,1280]{1,0:T(8,128)}) custom-call(bf16[56,1280]{1,0:T(8,128)(2,1)} %images_ref.1, bf16[56,1280]{1,0:T(8,128)(2,1)} %texts_ref.1, f32[1]{0:T(128)S(6)} %copy.9.scale_ref), custom_call_target="tpu_custom_call" | custom-call | tf_op jit(solution)/shard_map/pallas_call | solution.py:557
  68.4 0.0 copy-start
  68.4 1.7 %copy.11 = f32[56,1280]{1,0:T(8,128)} copy(f32[56,1280]{1,0:T(8,128)} %get-tuple-element.13) | data formatting | bytes 573440
  70.1 0.0 copy-done
  70.1 0.7 copy.12
Async XLA Ops:
  68.4 1.7 %copy-start = (f32[56,1280]{1,0:T(8,128)S(1)}, f32[56,1280]{1,0:T(8,128)}, u32[]{:S(2)}) copy-start(f32[56,1280]{1,0:T(8,128)} %get-tuple-element.14) | copy-start | bytes 860164
